TPU v7x, 256 devices: a whole 4x4x8 slice. The times are simulated.
256 devices in a mesh: fsdp: 64 (over y, x, z_hi), sp: 4 (over z_lo, core).
Axes of the slice: x: 4, y: 4, z: 8 (z_hi: 4, z_lo: 2; z = z_hi * 2 + z_lo), core: 2. Of those that a mesh axis runs over, the one named last changes fastest.
Arguments:
- gate_pre: bfloat16 [16384, 14848], P('fsdp', 'sp'), may hold values from -6 to 6
- up_pre: bfloat16 [16384, 14848], P('fsdp', 'sp'), may hold values from -6 to 6
- target_rows: bfloat16 [16384, 4096], P('fsdp'), may hold values from -6 to 6
- down_weight: bfloat16 [14848, 4096], P('sp', 'fsdp'), may hold values from -0.046875 to 0.046875
- old_logp: float32 [16384], P('fsdp'), may hold values from -3 to 3
- advantages: float32 [128], P('fsdp'), may hold values from -4 to 4
- lengths: int32 [128], P('fsdp'), may hold values from 32 to 112, as said below
- handoff: int32 [64], P('fsdp'), may hold values from 0 to 32, as said below
Outputs:
- gate_grad: bfloat16 [16384, 14848], P('fsdp', 'sp')
- up_grad: bfloat16 [16384, 14848], P('fsdp', 'sp')
- loss: float32 [], replicated
Inputs may be any that keep to these rules, and one draw needn't show every extreme that they name: `lengths`: two responses per index of fsdp, stored one after the other from the first of its 256 rows; the rows after them are padding. The first response has exactly 112 tokens. Index g of fsdp hands the last handoff[g] rows of its second response to index g + 1. The last index hands on nothing; index 0 and the next-to-last index hand on exactly 32.
All inputs are finite; a program needn't handle non-finite values.
Results may differ from a plain program's by a relative error of at most 0.0024.
Values may be sent and summed in bfloat16 or wider, within the bound.
No kernel may reach another device: no remote copies, remote signals or barrier semaphores. Data moves between devices by JAX's collectives and lax.ppermute only.
A program may use at most 128 MiB of HBM per device.

v0:
```python
import jax
import jax.numpy as jnp
from jax import lax
from jax.sharding import PartitionSpec as P

D = 4096


def passed_along(x, axis, by):
    peers = lax.axis_size(axis)
    pairs = [(i, i + by) for i in range(peers) if 0 <= i + by < peers]
    return lax.ppermute(x, axis, pairs)


def tail_rows(array, kept_rows, carried):
    return lax.dynamic_slice_in_dim(array, kept_rows, carried, 0)


def place_rows(array, arrived, kept_rows):
    return lax.dynamic_update_slice_in_dim(array, arrived, kept_rows, 0)


def shards(gate_pre, up_pre, target_rows, down_weight, old_logp, advantages, lengths, handoff):
    inv_root = 1.0 / D**0.5
    row_count = gate_pre.shape[0]
    carried = row_count // 8
    kept_rows = lengths[0] + lengths[1] - handoff[0]
    positions = jnp.arange(row_count, dtype=jnp.int32)
    in_first = positions < lengths[0]
    in_second = jnp.logical_and(positions >= lengths[0], positions < lengths[0] + lengths[1])
    live_mask = jnp.logical_or(in_first, in_second).astype(jnp.float32)
    row_adv = jnp.where(in_first, advantages[0], 0.0) + jnp.where(in_second, advantages[1], 0.0)
    count_part = jnp.sum(lengths).astype(jnp.float32)
    weight_full = lax.all_gather(down_weight, "fsdp", axis=1, tiled=True)
    probe_rows = (
        lax.dot_general(
            target_rows, weight_full, (((1,), (1,)), ((), ())), preferred_element_type=jnp.float32
        )
        * inv_root
    )
    gate_float = gate_pre.astype(jnp.float32)
    up_float = up_pre.astype(jnp.float32)
    sigmoid_gate = jax.nn.sigmoid(gate_float)
    activated = gate_float * sigmoid_gate
    partial_score = jnp.sum(activated * up_float * probe_rows, axis=1)
    token_score = lax.psum(partial_score, "sp")
    prob_ratio = jnp.exp(token_score - old_logp)
    plain_term = prob_ratio * row_adv
    clipped_term = jnp.clip(prob_ratio, 0.8, 1.2) * row_adv
    loss_part = jnp.sum(live_mask * jnp.minimum(plain_term, clipped_term))
    token_count, loss_sum = lax.psum((count_part, loss_part), "fsdp")
    loss_value = -loss_sum / token_count
    slope_row = jnp.where(plain_term <= clipped_term, -row_adv * prob_ratio, 0.0) * live_mask
    dhidden = slope_row[:, None] * probe_rows / token_count
    gate_grad = (
        dhidden * up_float * sigmoid_gate * (1.0 + gate_float * (1.0 - sigmoid_gate))
    ).astype(jnp.bfloat16)
    up_grad = (dhidden * activated).astype(jnp.bfloat16)
    arrived_grads = passed_along(
        (tail_rows(gate_grad, kept_rows, carried), tail_rows(up_grad, kept_rows, carried)),
        "fsdp",
        1,
    )
    gate_grad = place_rows(gate_grad, arrived_grads[0], kept_rows)
    up_grad = place_rows(up_grad, arrived_grads[1], kept_rows)
    return (gate_grad, up_grad, loss_value)


def solution(mesh):
    placed = (
        P("fsdp", "sp"),
        P("fsdp", "sp"),
        P("fsdp", None),
        P("sp", "fsdp"),
        P("fsdp"),
        P("fsdp"),
        P("fsdp"),
        P("fsdp"),
    )
    return jax.shard_map(
        shards,
        mesh=mesh,
        in_specs=placed,
        out_specs=(P("fsdp", "sp"), P("fsdp", "sp"), P()),
        check_vma=False,
    )
```

profile of v0, /device:TPU:0, one launch (start us, length us, event | category | flops | bytes accessed | tf_op | source)
XLA Modules:
  0.0 523.2 jit_solution(655360116049330721)
XLA Ops:
  7.2 0.0 copy-start
  7.2 0.0 all-gather.2.cloned.1.call-start
  7.2 0.7 all-gather.2.cloned.1.call-update
  8.6 1.3 reduce_sum.28
  10.5 1.3 fusion.13
  13.1 1.3 fusion.12
  14.4 0.0 copy-start.3
  14.4 261.9 %all-gather.2.cloned.1.call-done = bf16[3712,4096]{0,1:T(8,128)(2,1)} async-done(((bf16[3712,64]{0,1:T(8,128)(2,1)}), bf16[3712,4096]{0,1:T(8,128)(2,1)}) %all-gather.2.cloned.1.call-update) | async-done | bytes 30408720 | tf_op jit(solution)/shard_map/all_gather | solution.py:34
  276.4 0.0 copy-done
  276.4 16.8 %fusion.1 = (f32[256]{0:T(256)S(1)}, f32[256,3712]{1,0:T(8,128)}) fusion(bf16[256,3712]{1,0:T(8,128)(2,1)} %param.9, bf16[256,3712]{1,0:T(8,128)(2,1)} %param.8, bf16[256,4096]{1,0:T(8,128)(2,1)S(1)} %copy-done, bf16[3712,4096]{0,1:T(8,128)(2,1)} %all-gather.2.cloned.1.call-done), kind=kOutput, calls=%fused_computation.6 | convolution fusion | flops 7794130944 | bytes 40109056 | tf_op jit(solution)/shard_map/dot_general | solution.py:36
  293.2 6.6 %psum.21 = f32[256]{0:T(256)S(1)} all-reduce(f32[256]{0:T(256)S(1)} %get-tuple-element.13), channel_id=1, replica_groups=mesh['fsdp'=64,'sp'=4] {'sp'}, use_global_device_ids=true, to_apply=%region_1.2 | all-reduce | flops 256 | bytes 2048 | tf_op jit(solution)/shard_map/psum | solution.py:46
  299.7 0.0 copy-done.3
  299.7 2.6 fusion.10
  302.3 193.5 %all-reduce = (f32[]{:T(128)}, f32[]{:T(128)}) all-reduce(f32[]{:T(128)S(6)} %convert_element_type.18, f32[]{:T(128)} %get-tuple-element.8), channel_id=1, replica_groups=mesh['fsdp'=64,'sp'=4] {'fsdp'}, use_global_device_ids=true, to_apply=%region_3.4 | all-reduce | flops 2 | bytes 16 | tf_op jit(solution)/shard_map/psum | solution.py:51
  495.8 4.9 multiply_convert_fusion
  500.8 0.0 copy-start.1
  500.8 0.0 copy-start.2
  500.8 0.1 constant_dynamic-slice_fusion.1
  500.9 1.3 collective-permute-start
  502.2 0.0 copy-done.1
  502.2 0.1 constant_dynamic-slice_fusion
  502.3 0.4 copy-done.2
  502.6 1.3 collective-permute-start.1
  505.2 5.6 %collective-permute-done = bf16[32,3712]{1,0:T(8,128)(2,1)S(1)} collective-permute-done((bf16[32,3712]{1,0:T(8,128)(2,1)S(1)}, bf16[32,3712]{1,0:T(8,128)(2,1)S(1)}, u32[]{:S(2)}, u32[]{:S(2)}) %collective-permute-start) | collective-permute-done | bytes 237600 | tf_op jit(solution)/shard_map/ppermute | solution.py:12
  510.8 1.9 dynamic_update_slice.6
  512.7 0.6 collective-permute-done.1
  513.3 1.9 dynamic_update_slice.7
Async XLA Ops:
  7.2 269.2 %copy-start = (bf16[256,4096]{1,0:T(8,128)(2,1)S(1)}, bf16[256,4096]{1,0:T(8,128)(2,1)}, u32[]{:S(2)}) copy-start(bf16[256,4096]{1,0:T(8,128)(2,1)} %param.10) | copy-start | bytes 6291460
  7.2 269.2 %all-gather.2.cloned.1.call-start = ((), (), s32[]{:S(2)}) async-start(), calls=%async_computation | async-start | bytes 30883840 | tf_op jit(solution)/shard_map/all_gather | solution.py:34
  14.4 285.3 %copy-start.3 = (f32[256]{0:T(256)S(1)}, f32[256]{0:T(256)}, u32[]{:S(2)}) copy-start(f32[256]{0:T(256)} %param.12) | copy-start | bytes 3076
  500.8 1.4 copy-start.1
  500.8 1.9 copy-start.2
  500.9 9.9 %collective-permute-start = (bf16[32,3712]{1,0:T(8,128)(2,1)S(1)}, bf16[32,3712]{1,0:T(8,128)(2,1)S(1)}, u32[]{:S(2)}, u32[]{:S(2)}) collective-permute-start(bf16[32,3712]{1,0:T(8,128)(2,1)S(1)} %constant_dynamic-slice_fusion.1), channel_id=1, source_target_pairs={{0,4},{4,8},{8,12},{12,16},{16,20},{20,24},{24,28},{28,32},{32,36}... | collective-permute-start | bytes 712712 | tf_op jit(solution)/shard_map/ppermute | solution.py:12
  502.6 10.7 %collective-permute-start.1 = (bf16[32,3712]{1,0:T(8,128)(2,1)S(1)}, bf16[32,3712]{1,0:T(8,128)(2,1)S(1)}, u32[]{:S(2)}, u32[]{:S(2)}) collective-permute-start(bf16[32,3712]{1,0:T(8,128)(2,1)S(1)} %constant_dynamic-slice_fusion), channel_id=1, source_target_pairs={{0,4},{4,8},{8,12},{12,16},{16,20},{20,24},{24,28},{28,32},{32,36}... | collective-permute-start | bytes 712712 | tf_op jit(solution)/shard_map/ppermute | solution.py:12
Sparse Core Ops, SparseCore 0:
  11.3 265.0 all-gather.1
where the time goes:
time: 525 us; the launch traced here: 523 us
  waiting for transfers between devices  269 us (51%)
  blocking collectives  200 us (38%)
  between operations  19.1 us (4%)
  matrix products  16.8 us (3%)
  other arithmetic  8.79 us (2%)
  local copies, waits for them, and re-layouts  6.99 us (1%)
    all_gather x1, waiting for transfers between devices, shards(): weight_full = lax.all_gather(down_weight, 'fsdp', axis=1, tiled=True)  262 us
    psum x1, blocking collectives, shards(): token_count, loss_sum = lax.psum((count_part, loss_part), 'fsdp')  194 us
    dot_general x1, matrix products, shards(): lax.dot_general(target_rows, weight_full, (((1,), (1,)), ((), ())), prefe...  16.8 us
  transfers between devices with their start and end apart: 3, of which 3 were waited for; matrix products, arithmetic and copies ran while one was open for 1% of the time, Pallas kernels for 0%

commit v1 on v0

v1 whole, which is shorter than its diff:
```python
import functools

import jax
import jax.numpy as jnp
from jax import lax
from jax.experimental import pallas as pl
from jax.experimental.pallas import tpu as pltpu
from jax.sharding import Mesh, PartitionSpec as P

D = 4096
ROWS = 256
SPARE = 32
MINE = 3712
LANES = 128
STEP = 896
CHUNK = 1024
STAGES = 2
WIDE = CHUNK // STAGES
FS = ("y", "x", "h")
MIB = 1024 * 1024


def shift(value, axis, by):
    return lax.ppermute(value, axis, [(i, (i + by) % 4) for i in range(4)])


def mix(value, axis, bit):
    n = lax.axis_size(axis)
    return lax.ppermute(value, axis, [(i, i ^ bit) for i in range(n)])


def total(value):
    for axis in ("h", "x", "y"):
        value = (value + mix(value, axis, 1)) + (mix(value, axis, 2) + mix(value, axis, 3))
    return value


def relayed(array, kept, axis):
    tail = lax.dynamic_slice_in_dim(array, kept, SPARE, axis)
    tail = lax.ppermute(tail, FS, [(i, i + 1) for i in range(63)])
    return lax.dynamic_update_slice_in_dim(array, tail, kept, axis)


def ring(block, axis, forward):
    after = shift(block, axis, 1)
    before = shift(block, axis, -1)
    far = shift(after, axis, 1) if forward else shift(before, axis, -1)
    return [block, after, far, before]


def probe_kernel(pos, rows_ref, *refs):
    pieces, (out_ref, weight, sems) = refs[:16], refs[16:]

    @pl.when(pl.program_id(0) == 0)
    def _():
        copies = []
        for dy in range(4):
            for dh in range(4):
                k = dy * 4 + dh
                y = lax.rem(pos[1] + 4 - dy, 4)
                h = lax.rem(pos[2] + 4 - dh, 4)
                copy = pltpu.make_async_copy(pieces[k], weight.at[y, :, h], sems.at[k])
                copy.start()
                copies.append(copy)
        for copy in copies:
            copy.wait()

    product = jnp.dot(
        rows_ref[...], weight[...].reshape(D, WIDE), preferred_element_type=jnp.float32
    )
    out_ref[0] = product * (1.0 / D**0.5)


def probes(pos, rows, pieces):
    return pl.pallas_call(
        probe_kernel,
        grid_spec=pltpu.PrefetchScalarGridSpec(
            num_scalar_prefetch=1,
            grid=(4,),
            in_specs=[pl.BlockSpec((ROWS, D), lambda r, pos: (lax.rem(pos[0] + r, 4), 0))]
            + [pl.BlockSpec(memory_space=pl.ANY)] * 16,
            out_specs=pl.BlockSpec((1, ROWS, WIDE), lambda r, pos: (r, 0, 0)),
            scratch_shapes=[
                pltpu.VMEM((4, 4, 4, 64, WIDE), jnp.bfloat16),
                pltpu.SemaphoreType.DMA((16,)),
            ],
        ),
        out_shape=jax.ShapeDtypeStruct((4, ROWS, WIDE), jnp.float32),
        compiler_params=pltpu.CompilerParams(vmem_limit_bytes=48 * MIB),
        cost_estimate=pl.CostEstimate(
            flops=2 * 1024 * D * WIDE, bytes_accessed=2 * D * (1024 + WIDE), transcendentals=0
        ),
        name="probe",
    )(pos, rows, *pieces)


def tiles(pos):
    for k in range(4):
        member = lax.rem(pos[0] + 4 - k, 4)
        for s in range(STAGES):
            for t in range(WIDE // LANES):
                place = member * STEP + (s * WIDE + t * LANES)
                last = s == STAGES - 1 and t == WIDE // LANES - 1
                yield k * STAGES + s, t, pl.multiple_of(place, LANES), member, last


def part(ref, t):
    return ref[0, :, t * LANES : (t + 1) * LANES]


def score_kernel(pos, gate_ref, up_ref, *refs):
    pieces, out_ref = refs[:-1], refs[-1]
    acc = jnp.zeros((LANES, LANES), jnp.float32)
    for k, t, place, member, last in tiles(pos):
        gate = gate_ref[:, pl.ds(place, LANES)].astype(jnp.float32)
        up = up_ref[:, pl.ds(place, LANES)].astype(jnp.float32)
        term = gate * jax.nn.sigmoid(gate) * up * part(pieces[k], t)
        if last:
            term = jnp.where(member == 3, term, 0.0)
        acc = acc + term
    out_ref[0] = jnp.sum(acc.T, axis=0, keepdims=True)


def piece_specs(rows):
    return [pl.BlockSpec((1, rows, WIDE), lambda i, pos: (0, i, 0))] * (4 * STAGES)


def scores(pos, gate, up, pieces):
    wide = pl.BlockSpec((LANES, MINE), lambda i, pos: (i, 0))
    return pl.pallas_call(
        score_kernel,
        grid_spec=pltpu.PrefetchScalarGridSpec(
            num_scalar_prefetch=1,
            grid=(2,),
            in_specs=[wide, wide] + piece_specs(LANES),
            out_specs=pl.BlockSpec((1, 1, LANES), lambda i, pos: (i, 0, 0)),
        ),
        out_shape=jax.ShapeDtypeStruct((2, 1, LANES), jnp.float32),
        compiler_params=pltpu.CompilerParams(vmem_limit_bytes=48 * MIB),
        cost_estimate=pl.CostEstimate(
            flops=8 * ROWS * MINE, bytes_accessed=8 * ROWS * MINE, transcendentals=ROWS * MINE
        ),
        name="score",
    )(pos, gate, up, *pieces)


def slope_kernel(score_ref, info_ref, count_ref, slope_ref, loss_ref):
    loss = jnp.zeros((1, LANES), jnp.float32)
    for i in range(2):
        old = info_ref[0, i]
        adv = info_ref[1, i]
        mask = info_ref[2, i]
        ratio = jnp.exp(score_ref[i] - old)
        plain = ratio * adv
        clipped = jnp.clip(ratio, 0.8, 1.2) * adv
        loss = loss + mask * jnp.minimum(plain, clipped)
        slope = jnp.where(plain <= clipped, -adv * ratio, 0.0) * mask / count_ref[...]
        slope_ref[i * LANES : (i + 1) * LANES, :] = jnp.broadcast_to(slope, (LANES, LANES)).T
    loss_ref[...] = loss


def slopes(score, info, count):
    return pl.pallas_call(
        slope_kernel,
        out_shape=(
            jax.ShapeDtypeStruct((ROWS, LANES), jnp.float32),
            jax.ShapeDtypeStruct((1, LANES), jnp.float32),
        ),
        name="slope",
    )(score, info, count)


def grad_kernel(pos, gate_ref, up_ref, slope_ref, *refs):
    pieces, (gate_out, up_out) = refs[:-2], refs[-2:]
    slope = slope_ref[...]
    for k, t, place, _, _ in tiles(pos):
        here = pl.ds(place, LANES)
        gate = gate_ref[:, here].astype(jnp.float32)
        up = up_ref[:, here].astype(jnp.float32)
        sig = jax.nn.sigmoid(gate)
        dhidden = slope * part(pieces[k], t)
        gate_out[:, here] = (dhidden * up * sig * (1.0 + gate * (1.0 - sig))).astype(jnp.bfloat16)
        up_out[:, here] = (dhidden * (gate * sig)).astype(jnp.bfloat16)


def grads(pos, gate, up, slope, pieces):
    rows = 64
    wide = pl.BlockSpec((rows, MINE), lambda i, pos: (i, 0))
    return pl.pallas_call(
        grad_kernel,
        grid_spec=pltpu.PrefetchScalarGridSpec(
            num_scalar_prefetch=1,
            grid=(ROWS // rows,),
            in_specs=[wide, wide, pl.BlockSpec((rows, LANES), lambda i, pos: (i, 0))]
            + piece_specs(rows),
            out_specs=[wide, wide],
        ),
        out_shape=[jax.ShapeDtypeStruct((ROWS, MINE), jnp.bfloat16)] * 2,
        compiler_params=pltpu.CompilerParams(vmem_limit_bytes=48 * MIB),
        cost_estimate=pl.CostEstimate(
            flops=12 * ROWS * MINE, bytes_accessed=12 * ROWS * MINE, transcendentals=ROWS * MINE
        ),
        name="grad",
    )(pos, gate, up, slope, *pieces)


def shards(gate_pre, up_pre, target_rows, down_weight, old_logp, advantages, lengths, handoff):
    my_x = lax.axis_index("x")
    pos = jnp.stack([my_x, lax.axis_index("y"), lax.axis_index("h")]).astype(jnp.int32)
    kept = lengths[0] + lengths[1] - handoff[0]

    columns = down_weight.T
    sent = []
    for by in range(4):
        start = lax.rem(my_x + by, 4) * STEP
        chunk = lax.dynamic_slice_in_dim(columns, start, CHUNK, 1)
        sent.append(chunk if by == 0 else shift(chunk, "x", by))
    order = [lax.rem(my_x + 4 - x, 4) for x in range(4)]
    mine = jnp.stack([lax.select_n(k, *sent) for k in order])
    pieces = []
    for s in range(STAGES):
        block = mine[:, :, s * WIDE : (s + 1) * WIDE]
        near = ring(block, "h", s % 2 == 0)
        whole = [ring(b, "y", dh < 2) for dh, b in enumerate(near)]
        pieces.append([whole[dh][dy] for dy in range(4) for dh in range(4)])

    rows = relayed(target_rows, kept, 0)
    half = lax.dynamic_slice_in_dim(rows, lax.axis_index("c") * LANES, LANES, 0)
    group = lax.all_gather(half, ("x", "c"), axis=0, tiled=True)
    positions = jnp.arange(ROWS, dtype=jnp.int32)
    in_first = positions < lengths[0]
    in_second = jnp.logical_and(positions >= lengths[0], positions < lengths[0] + lengths[1])
    live = jnp.logical_or(in_first, in_second).astype(jnp.float32)
    adv = jnp.where(in_first, advantages[0], 0.0) + jnp.where(in_second, advantages[1], 0.0)
    info = relayed(jnp.stack([old_logp, adv, live]), kept, 1).reshape(3, 2, 1, LANES)
    gate = relayed(gate_pre, kept, 0)
    up = relayed(up_pre, kept, 0)
    count = total(jnp.full((1, LANES), jnp.sum(lengths).astype(jnp.float32)))

    home = [None] * (4 * STAGES)
    for s in range(STAGES):
        product = probes(pos, group, pieces[s])
        home[s] = product
        for by in range(1, 4):
            home[by * STAGES + s] = shift(product[by : by + 1], "x", by)
    partial = scores(pos, gate, up, home)
    score = partial + mix(partial, "c", 1)
    score = score + mix(score, "l", 1)
    slope, loss_part = slopes(score, info, count)
    gate_grad, up_grad = grads(pos, gate, up, slope, home)
    loss_sum = jnp.sum(total(loss_part))
    return gate_grad, up_grad, -loss_sum / count[0, 0]


def solution(mesh):
    grid = Mesh(mesh.devices.reshape(4, 4, 4, 2, 2), ("y", "x", "h", "l", "c"))
    sp = ("l", "c")
    return jax.shard_map(
        shards,
        mesh=grid,
        in_specs=(P(FS, sp), P(FS, sp), P(FS, None), P(sp, FS), P(FS), P(FS), P(FS), P(FS)),
        out_specs=(P(FS, sp), P(FS, sp), P()),
        check_vma=False,
    )
```

time: 525 us -> 285 us (0.54)
  waiting for transfers between devices: 269 us -> 47.8 us
  blocking collectives: 200 us -> 0 us
  starting transfers between devices: 2.63 us -> 141 us
  Pallas kernels: 0 us -> 32.5 us
  local copies, waits for them, and re-layouts: 6.99 us -> 32.9 us
  matrix products: 16.8 us -> 0 us
    all_gather x1, waiting for transfers between devices: 262 us -> 0.01 us  [shards(): group = lax.all_gather(half, ('x', 'c'), axis=0, tiled=True)]
    psum x2 -> x0, blocking collectives: 200 us -> none  [the longest x1 194 us: shards(): token_count, loss_sum = lax.psum((count_part, loss_part), 'fsdp')]
    ppermute x2 -> x63, starting transfers between devices: 2.6 us -> 141 us  [the longest x39 90.7 us: shift(): return lax.ppermute(value, axis, [(i, (i + by) % 4) for i in range(4)])]
    ppermute x2 -> x63, waiting for transfers between devices: 6.21 us -> 47.8 us  [the longest x39 30.1 us: shift(): return lax.ppermute(value, axis, [(i, (i + by) % 4) for i in range(4)])]
    pallas_call x0 -> x5, Pallas kernels: none -> 32.5 us  [the longest x2 20.9 us: probes(): pl.pallas_call(probe_kernel, grid_spec=pltpu.PrefetchScalarGridSpec(num_s...]
    dot_general x1 -> x0, matrix products: 16.8 us -> none  [shards(): lax.dot_general(target_rows, weight_full, (((1,), (1,)), ((), ())), prefe...]
    unnamed x8 -> x47, local copies, waits for them, and re-layouts: 0.4 us -> 13 us
    dynamic_slice x2 -> x6, local copies, waits for them, and re-layouts: 0.14 us -> 6.02 us  [the longest x4 3.69 us: relayed(): tail = lax.dynamic_slice_in_dim(array, kept, SPARE, axis)]
  transfers between devices with their start and end apart: 3 -> 64, of which waited for: 3 -> 19; matrix products, arithmetic and copies ran while one was open for 1% -> 6% of each run, Pallas kernels for 0% -> 11%
where the time goes in v1:
time: 285 us; the launch traced here: 279 us
  starting transfers between devices  141 us (49%)
  waiting for transfers between devices  47.8 us (17%)
  local copies, waits for them, and re-layouts  32.9 us (12%)
  Pallas kernels  32.5 us (11%)
  between operations  19.1 us (7%)
  other arithmetic  5.9 us (2%)
    ppermute x39, starting transfers between devices, shift(): return lax.ppermute(value, axis, [(i, (i + by) % 4) for i in range(4)])  90.7 us
    ppermute x20, starting transfers between devices, mix(): return lax.ppermute(value, axis, [(i, i ^ bit) for i in range(n)])  37.5 us
    ppermute x39, waiting for transfers between devices, shift(): return lax.ppermute(value, axis, [(i, (i + by) % 4) for i in range(4)])  30.1 us
    pallas_call x2, Pallas kernels, probes(): pl.pallas_call(probe_kernel, grid_spec=pltpu.PrefetchScalarGridSpec(num_s...  20.9 us
    ppermute x4, starting transfers between devices, relayed(): tail = lax.ppermute(tail, FS, [(i, i + 1) for i in range(63)])  13.1 us
    unnamed x47, local copies, waits for them, and re-layouts  13 us
    ppermute x20, waiting for transfers between devices, mix(): return lax.ppermute(value, axis, [(i, i ^ bit) for i in range(n)])  10.9 us
    dynamic_update_slice x4, local copies, waits for them, and re-layouts, relayed(): return lax.dynamic_update_slice_in_dim(array, tail, kept, axis)  7.05 us
  transfers between devices with their start and end apart: 64, of which 19 were waited for; matrix products, arithmetic and copies ran while one was open for 6% of the time, Pallas kernels for 11%

profile of v1, /device:TPU:0, one launch (start us, length us, event | category | flops | bytes accessed | tf_op | source)
XLA Modules:
  0.0 279.5 jit_solution(8420204476515709880)
XLA Ops:
  7.2 3.2 %copy.21 = bf16[256,4096]{1,0:T(8,128)(2,1)} copy(bf16[256,4096]{1,0:T(8,128)(2,1)} %param.10) | data formatting | bytes 4194304
  17.0 3.5 %collective-permute-start.2 = (bf16[32,4096]{1,0:T(8,128)(2,1)S(1)}, bf16[32,4096]{1,0:T(8,128)(2,1)S(1)}, u32[]{:S(2)}, u32[]{:S(2)}) collective-permute-start(bf16[32,4096]{1,0:T(8,128)(2,1)S(1)} %constant_dynamic-slice_fusion.2), channel_id=1, source_target_pairs={{0,4},{4,8},{8,12},{12,16},{16,20},{20,24},{24,28},{28,32},{32,36}... | collective-permute-start | bytes 786440 | tf_op jit(solution)/shard_map/ppermute | solution.py:40
  20.4 6.8 %collective-permute-done.2 = bf16[32,4096]{1,0:T(8,128)(2,1)S(1)} collective-permute-done((bf16[32,4096]{1,0:T(8,128)(2,1)S(1)}, bf16[32,4096]{1,0:T(8,128)(2,1)S(1)}, u32[]{:S(2)}, u32[]{:S(2)}) %collective-permute-start.2) | collective-permute-done | bytes 262176 | tf_op jit(solution)/shard_map/ppermute | solution.py:40
  32.3 6.1 %collective-permute-start.3 = (bf16[64,1024]{1,0:T(8,128)(2,1)S(1)}, bf16[64,1024]{1,0:T(8,128)(2,1)S(1)}, u32[]{:S(2)}, u32[]{:S(2)}) collective-permute-start(bf16[64,1024]{1,0:T(8,128)(2,1)S(1)} %get-tuple-element.24), channel_id=1, source_target_pairs={{0,16},{16,32},{32,48},{48,0},{1,17},{17,33},{33,49},{49,1},{2,18}... | collective-permute-start | bytes 393224 | tf_op jit(solution)/shard_map/ppermute | solution.py:24
  38.4 3.0 %collective-permute-start.4 = (bf16[64,1024]{1,0:T(8,128)(2,1)S(1)}, bf16[64,1024]{1,0:T(8,128)(2,1)S(1)}, u32[]{:S(2)}, u32[]{:S(2)}) collective-permute-start(bf16[64,1024]{1,0:T(8,128)(2,1)S(1)} %get-tuple-element.25), channel_id=1, source_target_pairs={{0,32},{16,48},{32,0},{48,16},{1,33},{17,49},{33,1},{49,17},{2,34}... | collective-permute-start | bytes 393224 | tf_op jit(solution)/shard_map/ppermute | solution.py:24
  46.8 6.0 %collective-permute-start.22 = (bf16[4,64,512]{2,1,0:T(8,128)(2,1)S(1)}, bf16[4,64,512]{2,1,0:T(8,128)(2,1)S(1)}, u32[]{:S(2)}, u32[]{:S(2)}) collective-permute-start(bf16[4,64,512]{2,1,0:T(8,128)(2,1)S(1)} %get-tuple-element.21.refs_0_), channel_id=1, source_target_pairs={{0,12},{4,0},{8,4},{12,8},{1,13},{5,1},{9,5},{13,9},{2,14},{6,2},{... | collective-permute-start | bytes 786440 | tf_op jit(solution)/shard_map/ppermute | solution.py:24
  56.1 3.4 %collective-permute-start.6 = (bf16[4,64,512]{2,1,0:T(8,128)(2,1)S(1)}, bf16[4,64,512]{2,1,0:T(8,128)(2,1)S(1)}, u32[]{:S(2)}, u32[]{:S(2)}) collective-permute-start(bf16[4,64,512]{2,1,0:T(8,128)(2,1)S(1)} %get-tuple-element.22.refs_0_), channel_id=1, source_target_pairs={{0,4},{4,8},{8,12},{12,0},{1,5},{5,9},{9,13},{13,1},{2,6},{6,10},{... | collective-permute-start | bytes 786440 | tf_op jit(solution)/shard_map/ppermute | solution.py:24
  59.4 3.4 %collective-permute-done.22.refs_3_ = bf16[4,64,512]{2,1,0:T(8,128)(2,1)S(1)} collective-permute-done((bf16[4,64,512]{2,1,0:T(8,128)(2,1)S(1)}, bf16[4,64,512]{2,1,0:T(8,128)(2,1)S(1)}, u32[]{:S(2)}, u32[]{:S(2)}) %collective-permute-start.22) | collective-permute-done | bytes 262176 | tf_op jit(solution)/shard_map/ppermute | solution.py:24
  62.8 7.5 %collective-permute-start.8 = (bf16[4,64,512]{2,1,0:T(8,128)(2,1)S(1)}, bf16[4,64,512]{2,1,0:T(8,128)(2,1)S(1)}, u32[]{:S(2)}, u32[]{:S(2)}) collective-permute-start(bf16[4,64,512]{2,1,0:T(8,128)(2,1)S(1)} %get-tuple-element.22.refs_0_), channel_id=1, source_target_pairs={{0,12},{4,0},{8,4},{12,8},{1,13},{5,1},{9,5},{13,9},{2,14},{6,2},{... | collective-permute-start | bytes 786440 | tf_op jit(solution)/shard_map/ppermute | solution.py:24
  75.4 3.6 %collective-permute-start.23 = (bf16[4,64,512]{2,1,0:T(8,128)(2,1)}, bf16[4,64,512]{2,1,0:T(8,128)(2,1)}, u32[]{:S(2)}, u32[]{:S(2)}) collective-permute-start(bf16[4,64,512]{2,1,0:T(8,128)(2,1)} %copy-done.3), channel_id=1, source_target_pairs={{0,12},{4,0},{8,4},{12,8},{1,13},{5,1},{9,5},{13,9},{2,14},{6,2},{... | collective-permute-start | bytes 786440 | tf_op jit(solution)/shard_map/ppermute | solution.py:24
  81.0 3.0 %collective-permute-start.32 = (bf16[4,64,512]{2,1,0:T(8,128)(2,1)}, bf16[4,64,512]{2,1,0:T(8,128)(2,1)}, u32[]{:S(2)}, u32[]{:S(2)}) collective-permute-start(bf16[4,64,512]{2,1,0:T(8,128)(2,1)} %copy-done.3), channel_id=1, source_target_pairs={{0,192},{64,0},{128,64},{192,128},{1,193},{65,1},{129,65},{193,129... | collective-permute-start | bytes 786440 | tf_op jit(solution)/shard_map/ppermute | solution.py:24
  95.9 4.5 %collective-permute-done.28.refs_8_ = bf16[4,64,512]{2,1,0:T(8,128)(2,1)S(1)} collective-permute-done((bf16[4,64,512]{2,1,0:T(8,128)(2,1)}, bf16[4,64,512]{2,1,0:T(8,128)(2,1)S(1)}, u32[]{:S(2)}, u32[]{:S(2)}) %collective-permute-start.28) | collective-permute-done | bytes 262176 | tf_op jit(solution)/shard_map/ppermute | solution.py:24
  101.8 3.2 %collective-permute-start.33 = (bf16[4,64,512]{2,1,0:T(8,128)(2,1)}, bf16[4,64,512]{2,1,0:T(8,128)(2,1)}, u32[]{:S(2)}, u32[]{:S(2)}) collective-permute-start(bf16[4,64,512]{2,1,0:T(8,128)(2,1)} %collective-permute-done.32.refs_15_), channel_id=1, source_target_pairs={{0,192},{64,0},{128,64},{192,128},{1,193},{65,1},{129,65},{193,129... | collective-permute-start | bytes 786440 | tf_op jit(solution)/shard_map/ppermute | solution.py:24
  113.3 3.7 %collective-permute-done.31.refs_10_ = bf16[4,64,512]{2,1,0:T(8,128)(2,1)} collective-permute-done((bf16[4,64,512]{2,1,0:T(8,128)(2,1)}, bf16[4,64,512]{2,1,0:T(8,128)(2,1)}, u32[]{:S(2)}, u32[]{:S(2)}) %collective-permute-start.31) | collective-permute-done | bytes 262176 | tf_op jit(solution)/shard_map/ppermute | solution.py:24
  117.0 3.0 %collective-permute-start.15 = (bf16[4,64,512]{2,1,0:T(8,128)(2,1)}, bf16[4,64,512]{2,1,0:T(8,128)(2,1)}, u32[]{:S(2)}, u32[]{:S(2)}) collective-permute-start(bf16[4,64,512]{2,1,0:T(8,128)(2,1)} %collective-permute-done.7.refs_2_), channel_id=1, source_target_pairs={{0,192},{64,0},{128,64},{192,128},{1,193},{65,1},{129,65},{193,129... | collective-permute-start | bytes 786440 | tf_op jit(solution)/shard_map/ppermute | solution.py:24
  123.8 10.7 %probe.3.refs_1_ = f32[4,256,512]{2,1,0:T(8,128)} custom-call(s32[3]{0:T(128)S(1)} %pad_add_fusion.pos, bf16[1024,4096]{1,0:T(8,128)(2,1)} %all-gather.2.cloned.1.call-done.rows_ref, bf16[4,64,512]{2,1,0:T(8,128)(2,1)S(1)} %get-tuple-element.21.refs_0_, bf16[4,64,512]{2,1,0:T(8,128)(2,1)} %collective-permute-done.21.refs_1_, ...), custom_call_target="tpu_custom_call" | custom-call | flops 4294967296 | bytes 12582912 | tf_op jit(solution)/shard_map/probe/pallas_call | solution.py:75
  134.5 9.1 %collective-permute-start.20 = (bf16[4,64,512]{2,1,0:T(8,128)(2,1)S(1)}, bf16[4,64,512]{2,1,0:T(8,128)(2,1)S(1)}, u32[]{:S(2)}, u32[]{:S(2)}) collective-permute-start(bf16[4,64,512]{2,1,0:T(8,128)(2,1)S(1)} %collective-permute-done.6.refs_1_), channel_id=1, source_target_pairs={{0,192},{64,0},{128,64},{192,128},{1,193},{65,1},{129,65},{193,129... | collective-permute-start | bytes 786440 | tf_op jit(solution)/shard_map/ppermute | solution.py:24
  145.6 3.2 %collective-permute-start.18 = (bf16[4,64,512]{2,1,0:T(8,128)(2,1)}, bf16[4,64,512]{2,1,0:T(8,128)(2,1)S(1)}, u32[]{:S(2)}, u32[]{:S(2)}) collective-permute-start(bf16[4,64,512]{2,1,0:T(8,128)(2,1)} %collective-permute-done.17.refs_15_), channel_id=1, source_target_pairs={{0,192},{64,0},{128,64},{192,128},{1,193},{65,1},{129,65},{193,129... | collective-permute-start | bytes 786440 | tf_op jit(solution)/shard_map/ppermute | solution.py:24
  152.1 4.1 %collective-permute-start.46 = (f32[1,128]{1,0:T(1,128)S(1)}, f32[1,128]{1,0:T(1,128)S(1)}, u32[]{:S(2)}, u32[]{:S(2)}) collective-permute-start(f32[1,128]{1,0:T(1,128)S(1)} %broadcast_in_dim.18), channel_id=1, source_target_pairs={{0,8},{4,12},{8,0},{12,4},{1,9},{5,13},{9,1},{13,5},{2,10},{6,14},... | collective-permute-start | bytes 1544 | tf_op jit(solution)/shard_map/ppermute | solution.py:29
  160.9 6.0 %collective-permute-start.37 = (f32[1,256,512]{2,1,0:T(8,128)S(1)}, f32[1,256,512]{2,1,0:T(8,128)S(1)}, u32[]{:S(2)}, u32[]{:S(2)}) collective-permute-start(f32[1,256,512]{2,1,0:T(8,128)S(1)} %get-tuple-element.13), channel_id=1, source_target_pairs={{0,16},{16,32},{32,48},{48,0},{1,17},{17,33},{33,49},{49,1},{2,18}... | collective-permute-start | bytes 1572872 | tf_op jit(solution)/shard_map/ppermute | solution.py:24
  166.9 10.3 %probe.2.refs_0_ = f32[4,256,512]{2,1,0:T(8,128)} custom-call(s32[3]{0:T(128)S(1)} %pad_add_fusion.pos, bf16[1024,4096]{1,0:T(8,128)(2,1)} %all-gather.2.cloned.1.call-done.rows_ref, bf16[4,64,512]{2,1,0:T(8,128)(2,1)S(1)} %get-tuple-element.22.refs_0_, bf16[4,64,512]{2,1,0:T(8,128)(2,1)S(1)} %collective-permute-done.6.refs_1_, ...), custom_call_target="tpu_custom_call" | custom-call | flops 4294967296 | bytes 12582912 | tf_op jit(solution)/shard_map/probe/pallas_call | solution.py:75
  177.2 3.0 %collective-permute-start = (bf16[32,3712]{1,0:T(8,128)(2,1)S(1)}, bf16[32,3712]{1,0:T(8,128)(2,1)S(1)}, u32[]{:S(2)}, u32[]{:S(2)}) collective-permute-start(bf16[32,3712]{1,0:T(8,128)(2,1)S(1)} %copy-done.15), channel_id=1, source_target_pairs={{0,4},{4,8},{8,12},{12,16},{16,20},{20,24},{24,28},{28,32},{32,36}... | collective-permute-start | bytes 712712 | tf_op jit(solution)/shard_map/ppermute | solution.py:40
  186.4 2.9 %collective-permute-start.38 = (f32[1,256,512]{2,1,0:T(8,128)}, f32[1,256,512]{2,1,0:T(8,128)}, u32[]{:S(2)}, u32[]{:S(2)}) collective-permute-start(f32[1,256,512]{2,1,0:T(8,128)} %get-tuple-element.15), channel_id=1, source_target_pairs={{0,32},{16,48},{32,0},{48,16},{1,33},{17,49},{33,1},{49,17},{2,34}... | collective-permute-start | bytes 1572872 | tf_op jit(solution)/shard_map/ppermute | solution.py:24
  199.6 3.8 %collective-permute-start.44 = (f32[3,32]{1,0:T(4,128)S(1)}, f32[3,32]{1,0:T(4,128)S(1)}, u32[]{:S(2)}, u32[]{:S(2)}) collective-permute-start(f32[3,32]{1,0:T(4,128)S(1)} %constant_dynamic-slice_fusion), channel_id=1, source_target_pairs={{0,4},{4,8},{8,12},{12,16},{16,20},{20,24},{24,28},{28,32},{32,36}... | collective-permute-start | bytes 1160 | tf_op jit(solution)/shard_map/ppermute | solution.py:40
  203.4 6.4 %collective-permute-done.41.refs_7_ = f32[1,256,512]{2,1,0:T(8,128)S(1)} collective-permute-done((f32[1,256,512]{2,1,0:T(8,128)}, f32[1,256,512]{2,1,0:T(8,128)S(1)}, u32[]{:S(2)}, u32[]{:S(2)}) %collective-permute-start.41) | collective-permute-done | bytes 524320 | tf_op jit(solution)/shard_map/ppermute | solution.py:24
  210.5 4.8 %collective-permute-start.49 = (f32[1,128]{1,0:T(1,128)S(1)}, f32[1,128]{1,0:T(1,128)S(1)}, u32[]{:S(2)}, u32[]{:S(2)}) collective-permute-start(f32[1,128]{1,0:T(1,128)S(1)} %add_add_fusion.4), channel_id=1, source_target_pairs={{0,32},{16,48},{32,0},{48,16},{1,33},{17,49},{33,1},{49,17},{2,34}... | collective-permute-start | bytes 1544 | tf_op jit(solution)/shard_map/ppermute | solution.py:29
  221.1 3.7 %score.1 = f32[2,1,128]{2,1,0:T(1,128)S(1)} custom-call(s32[3]{0:T(128)S(1)} %pad_add_fusion.pos, bf16[256,3712]{1,0:T(8,128)(2,1)S(1)} %dynamic_update_slice.12.gate_ref, bf16[256,3712]{1,0:T(8,128)(2,1)} %dynamic_update_slice.13.up_ref, f32[4,256,512]{2,1,0:T(8,128)} %probe.2.refs_0_, f32[4,256,512]{2,1,0:T(8,128)} %probe.3.refs_1_, ...), custom_call_target="tpu_custom_call" | custom-call | flops 7602176 | bytes 7602176 | tf_op jit(solution)/shard_map/score/pallas_call | solution.py:130
  238.1 4.8 %collective-permute-start.55 = (f32[1,128]{1,0:T(1,128)}, f32[1,128]{1,0:T(1,128)S(1)}, u32[]{:S(2)}, u32[]{:S(2)}) collective-permute-start(f32[1,128]{1,0:T(1,128)} %get-tuple-element.10), channel_id=1, source_target_pairs={{0,8},{4,12},{8,0},{12,4},{1,9},{5,13},{9,1},{13,5},{2,10},{6,14},... | collective-permute-start | bytes 1544 | tf_op jit(solution)/shard_map/ppermute | solution.py:29
  245.6 3.0 %collective-permute-done.56 = f32[1,128]{1,0:T(1,128)S(1)} collective-permute-done((f32[1,128]{1,0:T(1,128)}, f32[1,128]{1,0:T(1,128)S(1)}, u32[]{:S(2)}, u32[]{:S(2)}) %collective-permute-start.56) | collective-permute-done | bytes 544 | tf_op jit(solution)/shard_map/ppermute | solution.py:29
  249.4 3.6 %collective-permute-start.58 = (f32[1,128]{1,0:T(1,128)S(1)}, f32[1,128]{1,0:T(1,128)S(1)}, u32[]{:S(2)}, u32[]{:S(2)}) collective-permute-start(f32[1,128]{1,0:T(1,128)S(1)} %add_add_fusion.1), channel_id=1, source_target_pairs={{0,32},{16,48},{32,0},{48,16},{1,33},{17,49},{33,1},{49,17},{2,34}... | collective-permute-start | bytes 1544 | tf_op jit(solution)/shard_map/ppermute | solution.py:29
  254.6 3.2 %collective-permute-done.59 = f32[1,128]{1,0:T(1,128)S(1)} collective-permute-done((f32[1,128]{1,0:T(1,128)S(1)}, f32[1,128]{1,0:T(1,128)S(1)}, u32[]{:S(2)}, u32[]{:S(2)}) %collective-permute-start.59) | collective-permute-done | bytes 544 | tf_op jit(solution)/shard_map/ppermute | solution.py:29
  263.5 6.4 %grad.1 = (bf16[256,3712]{1,0:T(8,128)(2,1)}, bf16[256,3712]{1,0:T(8,128)(2,1)}) custom-call(s32[3]{0:T(128)S(1)} %pad_add_fusion.pos, bf16[256,3712]{1,0:T(8,128)(2,1)S(1)} %dynamic_update_slice.12.gate_ref, bf16[256,3712]{1,0:T(8,128)(2,1)} %dynamic_update_slice.13.up_ref, f32[256,128]{1,0:T(8,128)S(1)} %copy-done, f32[4,256,512]{2,1,0:T(8,128)} %probe.2.refs_0_, ...), custom_call_target="tpu_custom_call" | custom-call | flops 11403264 | bytes 11403264 | tf_op jit(solution)/shard_map/grad/pallas_call | solution.py:189
  (181 shorter events, 107.4 us)
Async XLA Ops:
  7.2 112.9 %all-gather.2.cloned.1.call-start = ((), (), s32[]{:S(2)}) async-start(), calls=%async_computation | async-start | bytes 9437184 | tf_op jit(solution)/shard_map/all_gather | solution.py:229
  46.8 16.0 %collective-permute-start.22 = (bf16[4,64,512]{2,1,0:T(8,128)(2,1)S(1)}, bf16[4,64,512]{2,1,0:T(8,128)(2,1)S(1)}, u32[]{:S(2)}, u32[]{:S(2)}) collective-permute-start(bf16[4,64,512]{2,1,0:T(8,128)(2,1)S(1)} %get-tuple-element.21.refs_0_), channel_id=1, source_target_pairs={{0,12},{4,0},{8,4},{12,8},{1,13},{5,1},{9,5},{13,9},{2,14},{6,2},{... | collective-permute-start | bytes 786440 | tf_op jit(solution)/shard_map/ppermute | solution.py:24
  52.8 19.4 %collective-permute-start.21 = (bf16[4,64,512]{2,1,0:T(8,128)(2,1)S(1)}, bf16[4,64,512]{2,1,0:T(8,128)(2,1)}, u32[]{:S(2)}, u32[]{:S(2)}) collective-permute-start(bf16[4,64,512]{2,1,0:T(8,128)(2,1)S(1)} %get-tuple-element.21.refs_0_), channel_id=1, source_target_pairs={{0,4},{4,8},{8,12},{12,0},{1,5},{5,9},{9,13},{13,1},{2,6},{6,10},{... | collective-permute-start | bytes 786440 | tf_op jit(solution)/shard_map/ppermute | solution.py:24
  52.8 21.1 %collective-permute-start.24 = (bf16[4,64,512]{2,1,0:T(8,128)(2,1)S(1)}, bf16[4,64,512]{2,1,0:T(8,128)(2,1)}, u32[]{:S(2)}, u32[]{:S(2)}) collective-permute-start(bf16[4,64,512]{2,1,0:T(8,128)(2,1)S(1)} %get-tuple-element.21.refs_0_), channel_id=1, source_target_pairs={{0,64},{64,128},{128,192},{192,0},{1,65},{65,129},{129,193},{193,1... | collective-permute-start | bytes 786440 | tf_op jit(solution)/shard_map/ppermute | solution.py:24
  54.4 21.0 %collective-permute-start.34 = (bf16[4,64,512]{2,1,0:T(8,128)(2,1)S(1)}, bf16[4,64,512]{2,1,0:T(8,128)(2,1)}, u32[]{:S(2)}, u32[]{:S(2)}) collective-permute-start(bf16[4,64,512]{2,1,0:T(8,128)(2,1)S(1)} %get-tuple-element.21.refs_0_), channel_id=1, source_target_pairs={{0,192},{64,0},{128,64},{192,128},{1,193},{65,1},{129,65},{193,129... | collective-permute-start | bytes 786440 | tf_op jit(solution)/shard_map/ppermute | solution.py:24
  56.1 23.0 %collective-permute-start.6 = (bf16[4,64,512]{2,1,0:T(8,128)(2,1)S(1)}, bf16[4,64,512]{2,1,0:T(8,128)(2,1)S(1)}, u32[]{:S(2)}, u32[]{:S(2)}) collective-permute-start(bf16[4,64,512]{2,1,0:T(8,128)(2,1)S(1)} %get-tuple-element.22.refs_0_), channel_id=1, source_target_pairs={{0,4},{4,8},{8,12},{12,0},{1,5},{5,9},{9,13},{13,1},{2,6},{6,10},{... | collective-permute-start | bytes 786440 | tf_op jit(solution)/shard_map/ppermute | solution.py:24
  62.8 18.1 %collective-permute-start.8 = (bf16[4,64,512]{2,1,0:T(8,128)(2,1)S(1)}, bf16[4,64,512]{2,1,0:T(8,128)(2,1)S(1)}, u32[]{:S(2)}, u32[]{:S(2)}) collective-permute-start(bf16[4,64,512]{2,1,0:T(8,128)(2,1)S(1)} %get-tuple-element.22.refs_0_), channel_id=1, source_target_pairs={{0,12},{4,0},{8,4},{12,8},{1,13},{5,1},{9,5},{13,9},{2,14},{6,2},{... | collective-permute-start | bytes 786440 | tf_op jit(solution)/shard_map/ppermute | solution.py:24
  84.9 16.2 %collective-permute-start.35 = (bf16[4,64,512]{2,1,0:T(8,128)(2,1)}, bf16[4,64,512]{2,1,0:T(8,128)(2,1)S(1)}, u32[]{:S(2)}, u32[]{:S(2)}) collective-permute-start(bf16[4,64,512]{2,1,0:T(8,128)(2,1)} %collective-permute-done.21.refs_1_), channel_id=1, source_target_pairs={{0,192},{64,0},{128,64},{192,128},{1,193},{65,1},{129,65},{193,129... | collective-permute-start | bytes 786440 | tf_op jit(solution)/shard_map/ppermute | solution.py:24
  87.5 12.9 %collective-permute-start.28 = (bf16[4,64,512]{2,1,0:T(8,128)(2,1)}, bf16[4,64,512]{2,1,0:T(8,128)(2,1)S(1)}, u32[]{:S(2)}, u32[]{:S(2)}) collective-permute-start(bf16[4,64,512]{2,1,0:T(8,128)(2,1)} %collective-permute-done.24.refs_4_), channel_id=1, source_target_pairs={{0,64},{64,128},{128,192},{192,0},{1,65},{65,129},{129,193},{193,1... | collective-permute-start | bytes 786440 | tf_op jit(solution)/shard_map/ppermute | solution.py:24
  90.3 14.7 %collective-permute-start.30 = (bf16[4,64,512]{2,1,0:T(8,128)(2,1)}, bf16[4,64,512]{2,1,0:T(8,128)(2,1)}, u32[]{:S(2)}, u32[]{:S(2)}) collective-permute-start(bf16[4,64,512]{2,1,0:T(8,128)(2,1)} %collective-permute-done.23.refs_2_), channel_id=1, source_target_pairs={{0,192},{64,0},{128,64},{192,128},{1,193},{65,1},{129,65},{193,129... | collective-permute-start | bytes 786440 | tf_op jit(solution)/shard_map/ppermute | solution.py:24
  92.1 15.6 %collective-permute-start.7 = (bf16[4,64,512]{2,1,0:T(8,128)(2,1)S(1)}, bf16[4,64,512]{2,1,0:T(8,128)(2,1)}, u32[]{:S(2)}, u32[]{:S(2)}) collective-permute-start(bf16[4,64,512]{2,1,0:T(8,128)(2,1)S(1)} %collective-permute-done.6.refs_1_), channel_id=1, source_target_pairs={{0,4},{4,8},{8,12},{12,0},{1,5},{5,9},{9,13},{13,1},{2,6},{6,10},{... | collective-permute-start | bytes 786440 | tf_op jit(solution)/shard_map/ppermute | solution.py:24
  95.6 14.1 %collective-permute-start.26 = (bf16[4,64,512]{2,1,0:T(8,128)(2,1)}, bf16[4,64,512]{2,1,0:T(8,128)(2,1)}, u32[]{:S(2)}, u32[]{:S(2)}) collective-permute-start(bf16[4,64,512]{2,1,0:T(8,128)(2,1)} %collective-permute-done.23.refs_2_), channel_id=1, source_target_pairs={{0,64},{64,128},{128,192},{192,0},{1,65},{65,129},{129,193},{193,1... | collective-permute-start | bytes 786440 | tf_op jit(solution)/shard_map/ppermute | solution.py:24
  107.7 26.8 %collective-permute-start.10 = (bf16[4,64,512]{2,1,0:T(8,128)(2,1)S(1)}, bf16[4,64,512]{2,1,0:T(8,128)(2,1)}, u32[]{:S(2)}, u32[]{:S(2)}) collective-permute-start(bf16[4,64,512]{2,1,0:T(8,128)(2,1)S(1)} %collective-permute-done.6.refs_1_), channel_id=1, source_target_pairs={{0,64},{64,128},{128,192},{192,0},{1,65},{65,129},{129,193},{193,1... | collective-permute-start | bytes 786440 | tf_op jit(solution)/shard_map/ppermute | solution.py:24
  109.7 34.0 %collective-permute-start.17 = (bf16[4,64,512]{2,1,0:T(8,128)(2,1)S(1)}, bf16[4,64,512]{2,1,0:T(8,128)(2,1)}, u32[]{:S(2)}, u32[]{:S(2)}) collective-permute-start(bf16[4,64,512]{2,1,0:T(8,128)(2,1)S(1)} %collective-permute-done.8.refs_3_), channel_id=1, source_target_pairs={{0,192},{64,0},{128,64},{192,128},{1,193},{65,1},{129,65},{193,129... | collective-permute-start | bytes 786440 | tf_op jit(solution)/shard_map/ppermute | solution.py:24
  110.9 34.6 %collective-permute-start.12 = (bf16[4,64,512]{2,1,0:T(8,128)(2,1)S(1)}, bf16[4,64,512]{2,1,0:T(8,128)(2,1)}, u32[]{:S(2)}, u32[]{:S(2)}) collective-permute-start(bf16[4,64,512]{2,1,0:T(8,128)(2,1)S(1)} %collective-permute-done.8.refs_3_), channel_id=1, source_target_pairs={{0,64},{64,128},{128,192},{192,0},{1,65},{65,129},{129,193},{193,1... | collective-permute-start | bytes 786440 | tf_op jit(solution)/shard_map/ppermute | solution.py:24
  111.7 33.9 %collective-permute-start.13 = (bf16[4,64,512]{2,1,0:T(8,128)(2,1)S(1)}, bf16[4,64,512]{2,1,0:T(8,128)(2,1)}, u32[]{:S(2)}, u32[]{:S(2)}) collective-permute-start(bf16[4,64,512]{2,1,0:T(8,128)(2,1)S(1)} %collective-permute-done.9.refs_4_), channel_id=1, source_target_pairs={{0,64},{64,128},{128,192},{192,0},{1,65},{65,129},{129,193},{193,1... | collective-permute-start | bytes 786440 | tf_op jit(solution)/shard_map/ppermute | solution.py:24
  117.0 31.8 %collective-permute-start.15 = (bf16[4,64,512]{2,1,0:T(8,128)(2,1)}, bf16[4,64,512]{2,1,0:T(8,128)(2,1)}, u32[]{:S(2)}, u32[]{:S(2)}) collective-permute-start(bf16[4,64,512]{2,1,0:T(8,128)(2,1)} %collective-permute-done.7.refs_2_), channel_id=1, source_target_pairs={{0,192},{64,0},{128,64},{192,128},{1,193},{65,1},{129,65},{193,129... | collective-permute-start | bytes 786440 | tf_op jit(solution)/shard_map/ppermute | solution.py:24
  134.5 16.9 %collective-permute-start.20 = (bf16[4,64,512]{2,1,0:T(8,128)(2,1)S(1)}, bf16[4,64,512]{2,1,0:T(8,128)(2,1)S(1)}, u32[]{:S(2)}, u32[]{:S(2)}) collective-permute-start(bf16[4,64,512]{2,1,0:T(8,128)(2,1)S(1)} %collective-permute-done.6.refs_1_), channel_id=1, source_target_pairs={{0,192},{64,0},{128,64},{192,128},{1,193},{65,1},{129,65},{193,129... | collective-permute-start | bytes 786440 | tf_op jit(solution)/shard_map/ppermute | solution.py:24
  145.6 12.3 %collective-permute-start.18 = (bf16[4,64,512]{2,1,0:T(8,128)(2,1)}, bf16[4,64,512]{2,1,0:T(8,128)(2,1)S(1)}, u32[]{:S(2)}, u32[]{:S(2)}) collective-permute-start(bf16[4,64,512]{2,1,0:T(8,128)(2,1)} %collective-permute-done.17.refs_15_), channel_id=1, source_target_pairs={{0,192},{64,0},{128,64},{192,128},{1,193},{65,1},{129,65},{193,129... | collective-permute-start | bytes 786440 | tf_op jit(solution)/shard_map/ppermute | solution.py:24
  151.4 25.8 %collective-permute-start.45 = (f32[1,128]{1,0:T(1,128)S(1)}, f32[1,128]{1,0:T(1,128)S(1)}, u32[]{:S(2)}, u32[]{:S(2)}) collective-permute-start(f32[1,128]{1,0:T(1,128)S(1)} %broadcast_in_dim.18), channel_id=1, source_target_pairs={{0,4},{4,0},{8,12},{12,8},{1,5},{5,1},{9,13},{13,9},{2,6},{6,2},{1... | collective-permute-start | bytes 1544 | tf_op jit(solution)/shard_map/ppermute | solution.py:29
  152.1 30.6 %collective-permute-start.46 = (f32[1,128]{1,0:T(1,128)S(1)}, f32[1,128]{1,0:T(1,128)S(1)}, u32[]{:S(2)}, u32[]{:S(2)}) collective-permute-start(f32[1,128]{1,0:T(1,128)S(1)} %broadcast_in_dim.18), channel_id=1, source_target_pairs={{0,8},{4,12},{8,0},{12,4},{1,9},{5,13},{9,1},{13,5},{2,10},{6,14},... | collective-permute-start | bytes 1544 | tf_op jit(solution)/shard_map/ppermute | solution.py:29
  156.3 27.5 %collective-permute-start.47 = (f32[1,128]{1,0:T(1,128)S(1)}, f32[1,128]{1,0:T(1,128)S(1)}, u32[]{:S(2)}, u32[]{:S(2)}) collective-permute-start(f32[1,128]{1,0:T(1,128)S(1)} %broadcast_in_dim.18), channel_id=1, source_target_pairs={{0,12},{4,8},{8,4},{12,0},{1,13},{5,9},{9,5},{13,1},{2,14},{6,10},... | collective-permute-start | bytes 1544 | tf_op jit(solution)/shard_map/ppermute | solution.py:29
  157.9 28.4 %collective-permute-start.1 = (bf16[32,3712]{1,0:T(8,128)(2,1)S(1)}, bf16[32,3712]{1,0:T(8,128)(2,1)S(1)}, u32[]{:S(2)}, u32[]{:S(2)}) collective-permute-start(bf16[32,3712]{1,0:T(8,128)(2,1)S(1)} %copy-done.14), channel_id=1, source_target_pairs={{0,4},{4,8},{8,12},{12,16},{16,20},{20,24},{24,28},{28,32},{32,36}... | collective-permute-start | bytes 712712 | tf_op jit(solution)/shard_map/ppermute | solution.py:40
  160.9 28.4 %collective-permute-start.37 = (f32[1,256,512]{2,1,0:T(8,128)S(1)}, f32[1,256,512]{2,1,0:T(8,128)S(1)}, u32[]{:S(2)}, u32[]{:S(2)}) collective-permute-start(f32[1,256,512]{2,1,0:T(8,128)S(1)} %get-tuple-element.13), channel_id=1, source_target_pairs={{0,16},{16,32},{32,48},{48,0},{1,17},{17,33},{33,49},{49,1},{2,18}... | collective-permute-start | bytes 1572872 | tf_op jit(solution)/shard_map/ppermute | solution.py:24
  182.7 16.9 %collective-permute-start.39 = (f32[1,256,512]{2,1,0:T(8,128)}, f32[1,256,512]{2,1,0:T(8,128)S(1)}, u32[]{:S(2)}, u32[]{:S(2)}) collective-permute-start(f32[1,256,512]{2,1,0:T(8,128)} %get-tuple-element.12), channel_id=1, source_target_pairs={{0,32},{16,48},{32,0},{48,16},{1,33},{17,49},{33,1},{49,17},{2,34}... | collective-permute-start | bytes 1572872 | tf_op jit(solution)/shard_map/ppermute | solution.py:24
  183.7 26.1 %collective-permute-start.41 = (f32[1,256,512]{2,1,0:T(8,128)}, f32[1,256,512]{2,1,0:T(8,128)S(1)}, u32[]{:S(2)}, u32[]{:S(2)}) collective-permute-start(f32[1,256,512]{2,1,0:T(8,128)} %get-tuple-element.11), channel_id=1, source_target_pairs={{0,48},{16,0},{32,16},{48,32},{1,49},{17,1},{33,17},{49,33},{2,50}... | collective-permute-start | bytes 1572872 | tf_op jit(solution)/shard_map/ppermute | solution.py:24
  186.3 24.2 %collective-permute-start.36 = (f32[1,256,512]{2,1,0:T(8,128)}, f32[1,256,512]{2,1,0:T(8,128)}, u32[]{:S(2)}, u32[]{:S(2)}) collective-permute-start(f32[1,256,512]{2,1,0:T(8,128)} %get-tuple-element.16), channel_id=1, source_target_pairs={{0,16},{16,32},{32,48},{48,0},{1,17},{17,33},{33,49},{49,1},{2,18}... | collective-permute-start | bytes 1572872 | tf_op jit(solution)/shard_map/ppermute | solution.py:24
  186.4 29.4 %collective-permute-start.38 = (f32[1,256,512]{2,1,0:T(8,128)}, f32[1,256,512]{2,1,0:T(8,128)}, u32[]{:S(2)}, u32[]{:S(2)}) collective-permute-start(f32[1,256,512]{2,1,0:T(8,128)} %get-tuple-element.15), channel_id=1, source_target_pairs={{0,32},{16,48},{32,0},{48,16},{1,33},{17,49},{33,1},{49,17},{2,34}... | collective-permute-start | bytes 1572872 | tf_op jit(solution)/shard_map/ppermute | solution.py:24
  189.3 31.8 %collective-permute-start.40 = (f32[1,256,512]{2,1,0:T(8,128)}, f32[1,256,512]{2,1,0:T(8,128)}, u32[]{:S(2)}, u32[]{:S(2)}) collective-permute-start(f32[1,256,512]{2,1,0:T(8,128)} %get-tuple-element.14), channel_id=1, source_target_pairs={{0,48},{16,0},{32,16},{48,32},{1,49},{17,1},{33,17},{49,33},{2,50}... | collective-permute-start | bytes 1572872 | tf_op jit(solution)/shard_map/ppermute | solution.py:24
  199.6 30.1 %collective-permute-start.44 = (f32[3,32]{1,0:T(4,128)S(1)}, f32[3,32]{1,0:T(4,128)S(1)}, u32[]{:S(2)}, u32[]{:S(2)}) collective-permute-start(f32[3,32]{1,0:T(4,128)S(1)} %constant_dynamic-slice_fusion), channel_id=1, source_target_pairs={{0,4},{4,8},{8,12},{12,16},{16,20},{20,24},{24,28},{28,32},{32,36}... | collective-permute-start | bytes 1160 | tf_op jit(solution)/shard_map/ppermute | solution.py:40
  209.8 15.1 %collective-permute-start.48 = (f32[1,128]{1,0:T(1,128)S(1)}, f32[1,128]{1,0:T(1,128)S(1)}, u32[]{:S(2)}, u32[]{:S(2)}) collective-permute-start(f32[1,128]{1,0:T(1,128)S(1)} %add_add_fusion.4), channel_id=1, source_target_pairs={{0,16},{16,0},{32,48},{48,32},{1,17},{17,1},{33,49},{49,33},{2,18}... | collective-permute-start | bytes 1544 | tf_op jit(solution)/shard_map/ppermute | solution.py:29
  210.5 14.4 %collective-permute-start.49 = (f32[1,128]{1,0:T(1,128)S(1)}, f32[1,128]{1,0:T(1,128)S(1)}, u32[]{:S(2)}, u32[]{:S(2)}) collective-permute-start(f32[1,128]{1,0:T(1,128)S(1)} %add_add_fusion.4), channel_id=1, source_target_pairs={{0,32},{16,48},{32,0},{48,16},{1,33},{17,49},{33,1},{49,17},{2,34}... | collective-permute-start | bytes 1544 | tf_op jit(solution)/shard_map/ppermute | solution.py:29
  (54 other events, 537.0 us)
Sparse Core Ops, SparseCore 0:
  32.4 60.8 all-gather.1

commit v2 on v1

v2 whole, which is shorter than its diff:
```python
import functools

import jax
import jax.numpy as jnp
from jax import lax
from jax.experimental import pallas as pl
from jax.experimental.pallas import tpu as pltpu
from jax.sharding import Mesh, PartitionSpec as P

D = 4096
ROWS = 256
SPARE = 32
MINE = 3712
LANES = 128
STEP = 896
CHUNK = 1024
FS = ("y", "x", "h")
CUTS = ((0, 512), (512, 512))
OWN, SIDE, OTHER, FAR = range(4)
MIB = 1024 * 1024


def swing(value, axis, way):
    pairs = []
    for i in range(4):
        for c in range(2):
            to = (i + {SIDE: 1 + 2 * c, OTHER: 3 + 2 * c, FAR: 2}[way]) % 4
            pairs.append((i * 2 + c, to * 2 + c))
    return lax.ppermute(value, (axis, "c"), pairs)


def mix(value, axis, bit):
    n = lax.axis_size(axis)
    return lax.ppermute(value, axis, [(i, i ^ bit) for i in range(n)])


def spread(value, axis):
    return (value + mix(value, axis, 1)) + (mix(value, axis, 2) + mix(value, axis, 3))


def tie(*values):
    return lax.optimization_barrier(values)


def onward(tail):
    return lax.ppermute(tail, FS, [(i, i + 1) for i in range(63)])


def moved(kept, own, tail):
    first = jnp.minimum(kept // 16 * 16, ROWS - 48)
    offset = kept - first
    window = pl.ds(pl.multiple_of(first, 16), 48)
    row = lax.broadcasted_iota(jnp.int32, (48, SPARE), 0)
    column = lax.broadcasted_iota(jnp.int32, (48, SPARE), 1)
    pick = (row == column + offset).astype(jnp.bfloat16)
    row = lax.broadcasted_iota(jnp.int32, (48, tail.shape[1]), 0)
    fresh = jnp.logical_and(row >= offset, row < offset + SPARE)
    new = jnp.dot(pick, tail, preferred_element_type=jnp.float32)
    return window, jnp.where(fresh, new, own[window, :].astype(jnp.float32)).astype(jnp.bfloat16)


def rows_kernel(where, own, tail, out_ref):
    out_ref[...] = own[...]
    window, new = moved(where[0], own, tail[...])
    out_ref[window, :] = new


def half_rows(where, rows, tail):
    return pl.pallas_call(
        rows_kernel,
        grid_spec=pltpu.PrefetchScalarGridSpec(
            num_scalar_prefetch=1,
            grid=(1,),
            in_specs=[
                pl.BlockSpec((ROWS, 2048), lambda i, where: (0, where[1])),
                pl.BlockSpec((SPARE, 2048), lambda i, where: (0, 0)),
            ],
            out_specs=pl.BlockSpec((ROWS, 2048), lambda i, where: (0, 0)),
        ),
        out_shape=jax.ShapeDtypeStruct((ROWS, 2048), jnp.bfloat16),
        compiler_params=pltpu.CompilerParams(vmem_limit_bytes=32 * MIB),
        name="rows",
    )(where, rows, tail)


def place_kernel(kept, gate, up, tails, gate_out, up_out):
    for own, tail, out in ((gate, tails[0], gate_out), (up, tails[1], up_out)):
        out[...] = own[...]
        window, new = moved(kept[0], own, tail)
        out[window, :] = new


def placed(kept, gate, up, tails):
    vmem = pl.BlockSpec(memory_space=pltpu.VMEM)
    return pl.pallas_call(
        place_kernel,
        in_specs=[pl.BlockSpec(memory_space=pltpu.SMEM)] + [vmem] * 3,
        out_specs=[vmem] * 2,
        out_shape=[jax.ShapeDtypeStruct((ROWS, MINE), jnp.bfloat16)] * 2,
        compiler_params=pltpu.CompilerParams(vmem_limit_bytes=60 * MIB),
        cost_estimate=pl.CostEstimate(flops=0, bytes_accessed=8 * ROWS * MINE, transcendentals=0),
        name="place",
    )(kept, gate, up, tails)


def start_all(pairs, sems):
    copies = [pltpu.make_async_copy(a, b, sems.at[k]) for k, (a, b) in enumerate(pairs)]
    for copy in copies:
        copy.start()
    return copies


def wait_all(copies):
    for copy in copies:
        copy.wait()


def probe_kernel(pos, rows_ref, *refs):
    parts, outs, (weight, rows, sems) = refs[:4], refs[4:8], refs[8:]
    waits = []
    for ky in range(4):
        half = pos[ky] // 2
        lanes = pl.ds(pl.multiple_of(lax.rem(pos[ky], 2) * 1024, 1024), 1024)
        pairs = [(parts[ky].at[k], weight.at[ky, :, pos[8 + k]]) for k in range(4)]
        for k in range(4):
            to = rows.at[ky, pl.ds(k * ROWS, ROWS)]
            pairs.append((rows_ref.at[pos[4 + k] * 2 + half, :, lanes], to))
        waits.append(start_all(pairs, sems.at[ky]))
    for ky in range(4):
        wait_all(waits[ky])
        product = jnp.dot(
            rows[ky], weight[ky].reshape(1024, -1), preferred_element_type=jnp.float32
        )
        for k in range(4):
            value = product[k * ROWS : (k + 1) * ROWS] * (1.0 / D**0.5)
            outs[k][...] = value if ky == 0 else outs[k][...] + value


def probes(pos, rows, parts):
    wide = parts[0].shape[-1]
    vmem = pl.BlockSpec(memory_space=pltpu.VMEM)
    return pl.pallas_call(
        probe_kernel,
        in_specs=[pl.BlockSpec(memory_space=pltpu.SMEM)] + [pl.BlockSpec(memory_space=pl.ANY)] * 5,
        out_specs=[vmem] * 4,
        scratch_shapes=[
            pltpu.VMEM((4, 4, 4, 64, wide), jnp.bfloat16),
            pltpu.VMEM((4, 4 * ROWS, 1024), jnp.bfloat16),
            pltpu.SemaphoreType.DMA((4, 8)),
        ],
        out_shape=[jax.ShapeDtypeStruct((ROWS, wide), jnp.float32)] * 4,
        compiler_params=pltpu.CompilerParams(vmem_limit_bytes=60 * MIB),
        cost_estimate=pl.CostEstimate(
            flops=8 * ROWS * D * wide, bytes_accessed=2 * D * (1024 + wide), transcendentals=0
        ),
        name="probe",
    )(pos, rows, *parts)


def tiles(pos):
    for k in range(4):
        member = pos[4 + k]
        for t in range(CHUNK // LANES):
            cut = max(i for i, (first, _) in enumerate(CUTS) if first <= t * LANES)
            there = t * LANES - CUTS[cut][0]
            place = pl.multiple_of(member * STEP + t * LANES, LANES)
            yield 4 * cut + k, slice(there, there + LANES), pl.ds(place, LANES), t, member


def score_kernel(pos, gate_ref, up_ref, *refs):
    pieces, out_ref = refs[:-1], refs[-1]
    acc = jnp.zeros((LANES, LANES), jnp.float32)
    for k, there, here, t, member in tiles(pos):
        gate = gate_ref[:, here].astype(jnp.float32)
        up = up_ref[:, here].astype(jnp.float32)
        term = gate * jax.nn.sigmoid(gate) * up * pieces[k][:, there]
        if t == CHUNK // LANES - 1:
            term = jnp.where(member == 3, term, 0.0)
        acc = acc + term
    out_ref[0] = jnp.sum(acc.T, axis=0, keepdims=True)


def piece_specs(rows):
    return [pl.BlockSpec((rows, n), lambda i, pos: (i, 0)) for _, n in CUTS for _ in range(4)]


def scores(pos, gate, up, pieces):
    wide = pl.BlockSpec((LANES, MINE), lambda i, pos: (i, 0))
    return pl.pallas_call(
        score_kernel,
        grid_spec=pltpu.PrefetchScalarGridSpec(
            num_scalar_prefetch=1,
            grid=(2,),
            in_specs=[wide, wide] + piece_specs(LANES),
            out_specs=pl.BlockSpec((1, 1, LANES), lambda i, pos: (i, 0, 0)),
        ),
        out_shape=jax.ShapeDtypeStruct((2, 1, LANES), jnp.float32),
        compiler_params=pltpu.CompilerParams(vmem_limit_bytes=60 * MIB),
        cost_estimate=pl.CostEstimate(
            flops=8 * ROWS * MINE, bytes_accessed=8 * ROWS * MINE, transcendentals=ROWS * MINE
        ),
        name="score",
    )(pos, gate, up, *pieces)


def info_kernel(nums, advs, old_ref, info_ref, tail_ref):
    at = lax.broadcasted_iota(jnp.int32, (1, ROWS), 1)
    in_first = at < nums[0]
    in_second = jnp.logical_and(at >= nums[0], at < nums[0] + nums[1])
    adv = jnp.where(in_first, advs[0], 0.0) + jnp.where(in_second, advs[1], 0.0)
    live = jnp.logical_or(in_first, in_second).astype(jnp.float32)
    row = lax.broadcasted_iota(jnp.int32, (8, ROWS), 0)
    info = jnp.where(row == 0, old_ref[...], jnp.where(row == 1, adv, live))
    info_ref[...] = info
    tail_ref[...] = pltpu.roll(info, ROWS - nums[2], 1)[:, :LANES]


def infos(nums, advs, old):
    smem = pl.BlockSpec(memory_space=pltpu.SMEM)
    return pl.pallas_call(
        info_kernel,
        in_specs=[smem, smem, pl.BlockSpec(memory_space=pltpu.VMEM)],
        out_shape=(
            jax.ShapeDtypeStruct((8, ROWS), jnp.float32),
            jax.ShapeDtypeStruct((8, LANES), jnp.float32),
        ),
        name="info",
    )(nums, advs, old)


def slope_kernel(nums, score_ref, info_ref, tail_ref, count_ref, slope_ref, loss_ref):
    at = lax.broadcasted_iota(jnp.int32, (8, ROWS), 1)
    fresh = jnp.logical_and(at >= nums[2], at < nums[2] + SPARE)
    tail = jnp.concatenate([tail_ref[...], tail_ref[...]], axis=1)
    info = jnp.where(fresh, pltpu.roll(tail, nums[2], 1), info_ref[...])
    loss = jnp.zeros((1, LANES), jnp.float32)
    for i in range(2):
        here = slice(i * LANES, (i + 1) * LANES)
        old, adv, mask = info[0:1, here], info[1:2, here], info[2:3, here]
        ratio = jnp.exp(score_ref[i] - old)
        plain = ratio * adv
        clipped = jnp.clip(ratio, 0.8, 1.2) * adv
        loss = loss + mask * jnp.minimum(plain, clipped)
        slope = jnp.where(plain <= clipped, -adv * ratio, 0.0) * mask / count_ref[...]
        slope_ref[here, :] = jnp.broadcast_to(slope, (LANES, LANES)).T
    loss_ref[...] = loss


def slopes(nums, score, info, tail, count):
    vmem = pl.BlockSpec(memory_space=pltpu.VMEM)
    return pl.pallas_call(
        slope_kernel,
        in_specs=[pl.BlockSpec(memory_space=pltpu.SMEM)] + [vmem] * 4,
        out_shape=(
            jax.ShapeDtypeStruct((ROWS, LANES), jnp.float32),
            jax.ShapeDtypeStruct((1, LANES), jnp.float32),
        ),
        name="slope",
    )(nums, score, info, tail, count)


def grad_kernel(pos, gate_ref, up_ref, slope_ref, *refs):
    pieces, (gate_out, up_out) = refs[:-2], refs[-2:]
    slope = slope_ref[...]
    for k, there, here, _, _ in tiles(pos):
        gate = gate_ref[:, here].astype(jnp.float32)
        up = up_ref[:, here].astype(jnp.float32)
        sig = jax.nn.sigmoid(gate)
        dhidden = slope * pieces[k][:, there]
        gate_out[:, here] = (dhidden * up * sig * (1.0 + gate * (1.0 - sig))).astype(jnp.bfloat16)
        up_out[:, here] = (dhidden * (gate * sig)).astype(jnp.bfloat16)


def grads(pos, gate, up, slope, pieces):
    rows = 64
    wide = pl.BlockSpec((rows, MINE), lambda i, pos: (i, 0))
    return pl.pallas_call(
        grad_kernel,
        grid_spec=pltpu.PrefetchScalarGridSpec(
            num_scalar_prefetch=1,
            grid=(ROWS // rows,),
            in_specs=[wide, wide, pl.BlockSpec((rows, LANES), lambda i, pos: (i, 0))]
            + piece_specs(rows),
            out_specs=[wide, wide],
        ),
        out_shape=[jax.ShapeDtypeStruct((ROWS, MINE), jnp.bfloat16)] * 2,
        compiler_params=pltpu.CompilerParams(vmem_limit_bytes=60 * MIB),
        cost_estimate=pl.CostEstimate(
            flops=12 * ROWS * MINE, bytes_accessed=12 * ROWS * MINE, transcendentals=ROWS * MINE
        ),
        name="grad",
    )(pos, gate, up, slope, *pieces)


def shards(gate_pre, up_pre, target_rows, down_weight, old_logp, advantages, lengths, handoff):
    at = {a: lax.axis_index(a) for a in ("y", "x", "h", "c")}
    ahead = [0, 1 + 2 * at["c"], 3 + 2 * at["c"], 2]
    behind = [0, 3 + 2 * at["c"], 1 + 2 * at["c"], 2]
    to_x = [lax.rem(at["x"] + k, 4) for k in ahead]
    from_x = [lax.rem(at["x"] + k, 4) for k in behind]
    kept = lengths[0] + lengths[1] - handoff[0]
    columns = down_weight.T
    chunks = [lax.dynamic_slice_in_dim(columns, x * STEP, CHUNK, 1) for x in to_x]
    chunks, target_rows, kept, lengths = tie(chunks, target_rows, kept, lengths)
    sent = [chunks[0]] + [swing(chunks[way], "x", way) for way in (SIDE, OTHER, FAR)]
    count = jnp.full((1, LANES), jnp.sum(lengths).astype(jnp.float32))
    tail = onward(lax.dynamic_slice(target_rows, (kept, at["c"] * 2048), (SPARE, 2048)))
    nums = jnp.stack([lengths[0], lengths[1], kept]).astype(jnp.int32)
    info, info_tail = infos(nums, advantages, old_logp.reshape(1, ROWS))
    info_tail = onward(info_tail)
    sent, lengths, kept, count, tail, info_tail = tie(
        sent, lengths, kept, count, tail, info_tail
    )
    mine = []
    for x in range(4):
        piece = sent[0]
        for k in (SIDE, OTHER, FAR):
            piece = jnp.where(from_x[k] == x, sent[k], piece)
        mine.append(piece)
    pos = [lax.rem(at["y"] + k, 4) for k in behind] + from_x
    pos = jnp.stack(pos + [lax.rem(at["h"] + k, 4) for k in behind]).astype(jnp.int32)

    block = jnp.stack(mine)
    block = [block[:, :, a : a + n] for a, n in CUTS]
    tails = jnp.stack([lax.dynamic_slice_in_dim(a, kept, SPARE, 0) for a in (gate_pre, up_pre)])

    def there(value, axis):
        return swing(value, axis, SIDE), swing(value, axis, OTHER)

    def again(side, axis):
        return swing(side, axis, SIDE)

    def returned(product):
        home = [product[OWN], None, None, None]
        for k, way in ((SIDE, OTHER), (OTHER, SIDE), (FAR, FAR)):
            home[way] = swing(product[k], "x", way)
        return home

    side, other = there(block[0], "h")
    side, other = tie(side, other)
    far = again(side, "h")
    where = jnp.stack([kept, at["c"]]).astype(jnp.int32)
    group = lax.all_gather(half_rows(where, target_rows, tail), ("x", "c"), axis=0)
    home, parts = [], None
    last = len(CUTS) - 1
    for i in range(last + 1):
        wide = jnp.stack([block[i], side, other, far])
        wide, block, parts, count = tie(wide, block, parts, count)
        a, b = there(wide, "y")
        if i < last:
            side, other = there(block[i + 1], "h")
        if i == 0:
            count = lax.psum(count, "x")
        product = probes(pos, group, parts) if i else None
        a, b, side, other, count, product, home, tails = tie(
            a, b, side, other, count, product, home, tails
        )
        if i:
            home = home + returned(product)
        c = again(a, "y")
        if i < last:
            far = again(side, "h")
        if i == last - 1:
            count = lax.psum(count, "h")
        parts = [wide, a, b, c]
    tails = onward(tails)
    product = probes(pos, group, parts)
    product, home, count, tails = tie(product, home, count, tails)
    home = home + returned(product)
    count = lax.psum(count, "y")
    gate, up = placed(kept.reshape(1).astype(jnp.int32), gate_pre, up_pre, tails)
    gate, up, count, home[-3], home[-2] = tie(gate, up, count, home[-3], home[-2])
    score = lax.psum(scores(pos, gate, up, home), ("l", "c"))
    slope, loss_part = slopes(nums, score, info, info_tail, count)
    loss_part = spread(loss_part, "h")
    gate_grad, up_grad = grads(pos, gate, up, slope, home)
    loss_part, gate_grad, up_grad = tie(loss_part, gate_grad, up_grad)
    loss_sum = jnp.sum(spread(spread(loss_part, "y"), "x"))
    return gate_grad, up_grad, -loss_sum / count[0, 0]


def solution(mesh):
    grid = Mesh(mesh.devices.reshape(4, 4, 4, 2, 2), ("y", "x", "h", "l", "c"))
    sp = ("l", "c")
    return jax.shard_map(
        shards,
        mesh=grid,
        in_specs=(P(FS, sp), P(FS, sp), P(FS, None), P(sp, FS), P(FS), P(FS), P(FS), P(FS)),
        out_specs=(P(FS, sp), P(FS, sp), P()),
        check_vma=False,
    )
```

time: 285 us -> 245 us (0.86); the launches traced: 279 us -> 242 us
  starting transfers between devices: 141 us -> 69.6 us
  blocking collectives: 0 us -> 51.5 us
  local copies, waits for them, and re-layouts: 32.9 us -> 10.7 us
  Pallas kernels: 32.5 us -> 39.5 us
    psum x0 -> x4, blocking collectives: none -> 51.5 us  [the longest x1 18.7 us: shards(): score = lax.psum(scores(pos, gate, up, home), ('l', 'c'))]
    ppermute x43 -> x24, starting transfers between devices: 104 us -> 53.6 us  [the longest x21 42.5 us: swing(): return lax.ppermute(value, (axis, 'c'), pairs)]
    ppermute x20 -> x9, starting transfers between devices: 37.5 us -> 16 us  [mix(): return lax.ppermute(value, axis, [(i, i ^ bit) for i in range(n)])]
    unnamed x47 -> x32, local copies, waits for them, and re-layouts: 13 us -> 5.34 us
    dynamic_update_slice x4 -> x0, local copies, waits for them, and re-layouts: 7.05 us -> none  [relayed(): return lax.dynamic_update_slice_in_dim(array, tail, kept, axis)]
    slice x4 -> x1, local copies, waits for them, and re-layouts: 5.63 us -> 0.06 us  [shards(): block = [block[:, :, a:a + n] for a, n in CUTS]]
    ppermute x20 -> x9, waiting for transfers between devices: 10.9 us -> 5.43 us  [mix(): return lax.ppermute(value, axis, [(i, i ^ bit) for i in range(n)])]
    ppermute x43 -> x24, waiting for transfers between devices: 36.9 us -> 41.9 us  [the longest x21 41.9 us: swing(): return lax.ppermute(value, (axis, 'c'), pairs)]
  transfers between devices with their start and end apart: 64 -> 34, of which waited for: 19 -> 13; matrix products, arithmetic and copies ran while one was open for 6% -> 2% of each run, Pallas kernels for 11% -> 13%
where the time goes in v2:
time: 245 us; the launch traced here: 242 us
  starting transfers between devices  69.6 us (28%)
  blocking collectives  51.5 us (21%)
  waiting for transfers between devices  47.4 us (19%)
  Pallas kernels  39.5 us (16%)
  between operations  18.9 us (8%)
  local copies, waits for them, and re-layouts  10.7 us (4%)
  other arithmetic  4.76 us (2%)
    ppermute x21, starting transfers between devices, swing(): return lax.ppermute(value, (axis, 'c'), pairs)  42.5 us
    ppermute x21, waiting for transfers between devices, swing(): return lax.ppermute(value, (axis, 'c'), pairs)  41.9 us
    psum x1, blocking collectives, shards(): score = lax.psum(scores(pos, gate, up, home), ('l', 'c'))  18.7 us
    pallas_call x2, Pallas kernels, probes(): pl.pallas_call(probe_kernel, in_specs=[pl.BlockSpec(memory_space=pltpu.SM...  18 us
    ppermute x9, starting transfers between devices, mix(): return lax.ppermute(value, axis, [(i, i ^ bit) for i in range(n)])  16 us
    psum x1, blocking collectives, shards(): count = lax.psum(count, 'h')  15.8 us
    ppermute x3, starting transfers between devices, onward(): return lax.ppermute(tail, FS, [(i, i + 1) for i in range(63)])  11.1 us
    psum x1, blocking collectives, shards(): count = lax.psum(count, 'y')  9.16 us
  transfers between devices with their start and end apart: 34, of which 13 were waited for; matrix products, arithmetic and copies ran while one was open for 2% of the time, Pallas kernels for 13%

profile of v2, /device:TPU:0, one launch (start us, length us, event | category | flops | bytes accessed | tf_op | source)
XLA Modules:
  0.0 242.4 jit_solution(3659856776451620896)
XLA Ops:
  12.7 3.4 %collective-permute-start.3 = (bf16[32,2048]{1,0:T(8,128)(2,1)S(1)}, bf16[32,2048]{1,0:T(8,128)(2,1)S(1)}, u32[]{:S(2)}, u32[]{:S(2)}) collective-permute-start(bf16[32,2048]{1,0:T(8,128)(2,1)S(1)} %dynamic_slice.25), channel_id=1, source_target_pairs={{0,4},{4,8},{8,12},{12,16},{16,20},{20,24},{24,28},{28,32},{32,36}... | collective-permute-start | bytes 393224 | tf_op jit(solution)/shard_map/ppermute | solution.py:46
  24.0 6.4 %collective-permute-start.4 = (f32[8,128]{1,0:T(8,128)}, f32[8,128]{1,0:T(8,128)S(1)}, u32[]{:S(2)}, u32[]{:S(2)}) collective-permute-start(f32[8,128]{1,0:T(8,128)} %get-tuple-element.84), channel_id=1, source_target_pairs={{0,4},{4,8},{8,12},{12,16},{16,20},{20,24},{24,28},{28,32},{32,36}... | collective-permute-start | bytes 12296 | tf_op jit(solution)/shard_map/ppermute | solution.py:46
  36.0 2.8 %collective-permute-start.5 = (bf16[4,64,512]{2,1,0:T(8,128)(2,1)S(1)}, bf16[4,64,512]{2,1,0:T(8,128)(2,1)S(1)}, u32[]{:S(2)}, u32[]{:S(2)}) collective-permute-start(bf16[4,64,512]{2,1,0:T(8,128)(2,1)S(1)} %get-tuple-element.153), channel_id=1, source_target_pairs={{0,4},{1,13},{4,8},{5,1},{8,12},{9,5},{12,0},{13,9},{2,6},{3,15},{... | collective-permute-start | bytes 786440 | tf_op jit(solution)/shard_map/ppermute | solution.py:29
  40.3 6.4 %collective-permute-done.5 = bf16[4,64,512]{2,1,0:T(8,128)(2,1)S(1)} collective-permute-done((bf16[4,64,512]{2,1,0:T(8,128)(2,1)S(1)}, bf16[4,64,512]{2,1,0:T(8,128)(2,1)S(1)}, u32[]{:S(2)}, u32[]{:S(2)}) %collective-permute-start.5) | collective-permute-done | bytes 262176 | tf_op jit(solution)/shard_map/ppermute | solution.py:29
  46.6 2.6 %collective-permute-done.6 = bf16[4,64,512]{2,1,0:T(8,128)(2,1)S(1)} collective-permute-done((bf16[4,64,512]{2,1,0:T(8,128)(2,1)S(1)}, bf16[4,64,512]{2,1,0:T(8,128)(2,1)S(1)}, u32[]{:S(2)}, u32[]{:S(2)}) %collective-permute-start.6) | collective-permute-done | bytes 262176 | tf_op jit(solution)/shard_map/ppermute | solution.py:29
  49.3 4.2 %collective-permute-start.7 = (bf16[4,64,512]{2,1,0:T(8,128)(2,1)S(1)}, bf16[4,64,512]{2,1,0:T(8,128)(2,1)S(1)}, u32[]{:S(2)}, u32[]{:S(2)}) collective-permute-start(bf16[4,64,512]{2,1,0:T(8,128)(2,1)S(1)} %collective-permute-done.5), channel_id=1, source_target_pairs={{0,4},{1,13},{4,8},{5,1},{8,12},{9,5},{12,0},{13,9},{2,6},{3,15},{... | collective-permute-start | bytes 786440 | tf_op jit(solution)/shard_map/ppermute | solution.py:29
  53.5 6.7 %collective-permute-done.7 = bf16[4,64,512]{2,1,0:T(8,128)(2,1)S(1)} collective-permute-done((bf16[4,64,512]{2,1,0:T(8,128)(2,1)S(1)}, bf16[4,64,512]{2,1,0:T(8,128)(2,1)S(1)}, u32[]{:S(2)}, u32[]{:S(2)}) %collective-permute-start.7) | collective-permute-done | bytes 262176 | tf_op jit(solution)/shard_map/ppermute | solution.py:29
  60.4 3.8 %collective-permute-start.8 = (bf16[4,4,64,512]{3,2,1,0:T(8,128)(2,1)S(1)}, bf16[4,4,64,512]{3,2,1,0:T(8,128)(2,1)}, u32[]{:S(2)}, u32[]{:S(2)}) collective-permute-start(bf16[4,4,64,512]{3,2,1,0:T(8,128)(2,1)S(1)} %pad_maximum_fusion.refs_0_), channel_id=1, source_target_pairs={{0,64},{1,193},{64,128},{65,1},{128,192},{129,65},{192,0},{193,129... | collective-permute-start | bytes 3145736 | tf_op jit(solution)/shard_map/ppermute | solution.py:29
  68.3 2.7 %collective-permute-start.11 = (bf16[4,64,512]{2,1,0:T(8,128)(2,1)S(1)}, bf16[4,64,512]{2,1,0:T(8,128)(2,1)S(1)}, u32[]{:S(2)}, u32[]{:S(2)}) collective-permute-start(bf16[4,64,512]{2,1,0:T(8,128)(2,1)S(1)} %get-tuple-element.94), channel_id=1, source_target_pairs={{0,12},{1,5},{4,0},{5,9},{8,4},{9,13},{12,8},{13,1},{2,14},{3,7},{... | collective-permute-start | bytes 786440 | tf_op jit(solution)/shard_map/ppermute | solution.py:29
  71.1 7.9 %psum.28 = f32[1,128]{1,0:T(1,128)S(1)} all-reduce(f32[1,128]{1,0:T(1,128)S(1)} %broadcast_in_dim.3), channel_id=1, replica_groups=mesh['y'=4,'x'=4,'h'=4,'l'=2,'c'=2] {'x'}, use_global_device_ids=true, to_apply=%region_1.2 | all-reduce | flops 128 | bytes 1024 | tf_op jit(solution)/shard_map/psum | solution.py:353
  79.1 4.2 %collective-permute-done.8.refs_1_ = bf16[4,4,64,512]{3,2,1,0:T(8,128)(2,1)} collective-permute-done((bf16[4,4,64,512]{3,2,1,0:T(8,128)(2,1)S(1)}, bf16[4,4,64,512]{3,2,1,0:T(8,128)(2,1)}, u32[]{:S(2)}, u32[]{:S(2)}) %collective-permute-start.8) | collective-permute-done | bytes 1048608 | tf_op jit(solution)/shard_map/ppermute | solution.py:29
  85.0 15.8 %psum.29 = f32[1,128]{1,0:T(1,128)S(1)} all-reduce(f32[1,128]{1,0:T(1,128)S(1)} %psum.28), channel_id=1, replica_groups=mesh['y'=4,'x'=4,'h'=4,'l'=2,'c'=2] {'h'}, use_global_device_ids=true, to_apply=%region_2.3 | all-reduce | flops 128 | bytes 1024 | tf_op jit(solution)/shard_map/psum | solution.py:364
  103.3 2.0 collective-permute-start.15
  105.9 8.9 %probe.2 = (f32[256,512]{1,0:T(8,128)}, f32[256,512]{1,0:T(8,128)}, f32[256,512]{1,0:T(8,128)}, f32[256,512]{1,0:T(8,128)}) custom-call(s32[12]{0:T(128)} %stack.120.pos, bf16[8,256,2048]{2,1,0:T(8,128)(2,1)} %bitcast.57, bf16[4,4,64,512]{3,2,1,0:T(8,128)(2,1)} %copy-done.7, bf16[4,4,64,512]{3,2,1,0:T(8,128)(2,1)} %collective-permute-done.8.refs_1_, ...), custom_call_target="tpu_custom_call" | custom-call | flops 4294967296 | bytes 12582912 | tf_op jit(solution)/shard_map/probe/pallas_call | solution.py:142
  114.9 7.2 %collective-permute-done.14.refs_1_ = bf16[4,4,64,512]{3,2,1,0:T(8,128)(2,1)} collective-permute-done((bf16[4,4,64,512]{3,2,1,0:T(8,128)(2,1)S(1)}, bf16[4,4,64,512]{3,2,1,0:T(8,128)(2,1)}, u32[]{:S(2)}, u32[]{:S(2)}) %collective-permute-start.14) | collective-permute-done | bytes 1048608 | tf_op jit(solution)/shard_map/ppermute | solution.py:29
  123.1 2.4 collective-permute-start.17
  127.4 4.6 %collective-permute-start.19 = (f32[256,512]{1,0:T(8,128)}, f32[256,512]{1,0:T(8,128)S(1)}, u32[]{:S(2)}, u32[]{:S(2)}) collective-permute-start(f32[256,512]{1,0:T(8,128)} %get-tuple-element.122), channel_id=1, source_target_pairs={{0,32},{1,33},{16,48},{17,49},{32,0},{33,1},{48,16},{49,17},{2,34}... | collective-permute-start | bytes 1572872 | tf_op jit(solution)/shard_map/ppermute | solution.py:29
  133.3 7.5 %collective-permute-done.16.refs_3_ = bf16[4,4,64,512]{3,2,1,0:T(8,128)(2,1)S(1)} collective-permute-done((bf16[4,4,64,512]{3,2,1,0:T(8,128)(2,1)}, bf16[4,4,64,512]{3,2,1,0:T(8,128)(2,1)S(1)}, u32[]{:S(2)}, u32[]{:S(2)}) %collective-permute-start.16) | collective-permute-done | bytes 1048608 | tf_op jit(solution)/shard_map/ppermute | solution.py:29
  141.8 9.1 %probe.3 = (f32[256,512]{1,0:T(8,128)}, f32[256,512]{1,0:T(8,128)}, f32[256,512]{1,0:T(8,128)}, f32[256,512]{1,0:T(8,128)}) custom-call(s32[12]{0:T(128)} %stack.120.pos, bf16[8,256,2048]{2,1,0:T(8,128)(2,1)} %bitcast.58, bf16[4,4,64,512]{3,2,1,0:T(8,128)(2,1)} %copy-done.8, bf16[4,4,64,512]{3,2,1,0:T(8,128)(2,1)} %collective-permute-done.14.refs_1_, ...), custom_call_target="tpu_custom_call" | custom-call | flops 4294967296 | bytes 12582912 | tf_op jit(solution)/shard_map/probe/pallas_call | solution.py:142
  150.9 4.9 %collective-permute-done.19.refs_3_ = f32[256,512]{1,0:T(8,128)S(1)} collective-permute-done((f32[256,512]{1,0:T(8,128)}, f32[256,512]{1,0:T(8,128)S(1)}, u32[]{:S(2)}, u32[]{:S(2)}) %collective-permute-start.19) | collective-permute-done | bytes 524320 | tf_op jit(solution)/shard_map/ppermute | solution.py:29
  155.8 3.2 %collective-permute-start.22 = (f32[256,512]{1,0:T(8,128)}, f32[256,512]{1,0:T(8,128)S(1)}, u32[]{:S(2)}, u32[]{:S(2)}) collective-permute-start(f32[256,512]{1,0:T(8,128)} %get-tuple-element.130), channel_id=1, source_target_pairs={{0,48},{1,17},{16,0},{17,33},{32,16},{33,49},{48,32},{49,1},{2,50}... | collective-permute-start | bytes 1572872 | tf_op jit(solution)/shard_map/ppermute | solution.py:29
  159.0 2.3 collective-permute-start.23
  161.3 4.4 %place.1 = (bf16[256,3712]{1,0:T(8,128)(2,1)}, bf16[256,3712]{1,0:T(8,128)(2,1)}) custom-call(s32[1]{0:T(128)} %bitcast.19.kept, bf16[256,3712]{1,0:T(8,128)(2,1)} %gate.1, bf16[256,3712]{1,0:T(8,128)(2,1)} %up.1, bf16[2,32,3712]{2,1,0:T(8,128)(2,1)} %copy-done.9), custom_call_target="tpu_custom_call" | custom-call | bytes 7602176 | tf_op jit(solution)/shard_map/place/pallas_call | solution.py:95
  165.7 9.2 %psum.30.count_ref = f32[1,128]{1,0:T(1,128)} all-reduce(f32[1,128]{1,0:T(1,128)S(1)} %psum.29), channel_id=1, replica_groups=mesh['y'=4,'x'=4,'h'=4,'l'=2,'c'=2] {'y'}, use_global_device_ids=true, to_apply=%region_3.4 | all-reduce | flops 128 | bytes 1024 | tf_op jit(solution)/shard_map/psum | solution.py:370
  174.9 2.2 collective-permute-done.21.refs_5_
  178.8 5.2 %score.1 = f32[2,1,128]{2,1,0:T(1,128)} custom-call(s32[12]{0:T(128)} %stack.120.pos, bf16[256,3712]{1,0:T(8,128)(2,1)} %get-tuple-element.131.gate_ref, bf16[256,3712]{1,0:T(8,128)(2,1)} %get-tuple-element.132.up_ref, f32[256,512]{1,0:T(8,128)} %get-tuple-element.133.refs_0_, f32[256,512]{1,0:T(8,128)} %copy-done.1, f32[256,512]{1,0:T(8,128)} %copy-done.2, ...), custom_call_target="tpu_custom_call" | custom-call | flops 7602176 | bytes 7602176 | tf_op jit(solution)/shard_map/score/pallas_call | solution.py:189
  184.0 18.7 %psum.31.score_ref = f32[2,1,128]{2,1,0:T(1,128)} all-reduce(f32[2,1,128]{2,1,0:T(1,128)} %score.1), channel_id=1, replica_groups=mesh['y'=4,'x'=4,'h'=4,'l'=2,'c'=2] {'l','c'}, use_global_device_ids=true, to_apply=%region_4.5 | all-reduce | flops 256 | bytes 2048 | tf_op jit(solution)/shard_map/psum | solution.py:373
  204.3 6.5 %collective-permute-start.26 = (f32[1,128]{1,0:T(1,128)}, f32[1,128]{1,0:T(1,128)S(1)}, u32[]{:S(2)}, u32[]{:S(2)}) collective-permute-start(f32[1,128]{1,0:T(1,128)} %get-tuple-element.144), channel_id=1, source_target_pairs={{0,12},{4,8},{8,4},{12,0},{1,13},{5,9},{9,5},{13,1},{2,14},{6,10},... | collective-permute-start | bytes 1544 | tf_op jit(solution)/shard_map/ppermute | solution.py:34
  210.8 7.2 %grad.1 = (bf16[256,3712]{1,0:T(8,128)(2,1)}, bf16[256,3712]{1,0:T(8,128)(2,1)}) custom-call(s32[12]{0:T(128)} %stack.120.pos, bf16[256,3712]{1,0:T(8,128)(2,1)} %get-tuple-element.131.gate_ref, bf16[256,3712]{1,0:T(8,128)(2,1)} %get-tuple-element.132.up_ref, f32[256,128]{1,0:T(8,128)} %get-tuple-element.145.slope_ref, ...), custom_call_target="tpu_custom_call" | custom-call | flops 11403264 | bytes 11403264 | tf_op jit(solution)/shard_map/grad/pallas_call | solution.py:277
  222.9 2.1 collective-permute-done.28
  226.2 2.1 collective-permute-start.31
  228.3 2.6 %collective-permute-start.32 = (f32[1,128]{1,0:T(1,128)S(1)}, f32[1,128]{1,0:T(1,128)S(1)}, u32[]{:S(2)}, u32[]{:S(2)}) collective-permute-start(f32[1,128]{1,0:T(1,128)S(1)} %add_add_fusion), channel_id=1, source_target_pairs={{0,48},{16,32},{32,16},{48,0},{1,49},{17,33},{33,17},{49,1},{2,50}... | collective-permute-start | bytes 1544 | tf_op jit(solution)/shard_map/ppermute | solution.py:34
  (99 shorter events, 44.4 us)
Async XLA Ops:
  7.2 98.8 %all-gather.3.cloned.1.call-start = ((), (), s32[]{:S(2)}) async-start(), calls=%async_computation | async-start | bytes 9437184 | tf_op jit(solution)/shard_map/all_gather | solution.py:343
  12.7 19.6 %collective-permute-start.3 = (bf16[32,2048]{1,0:T(8,128)(2,1)S(1)}, bf16[32,2048]{1,0:T(8,128)(2,1)S(1)}, u32[]{:S(2)}, u32[]{:S(2)}) collective-permute-start(bf16[32,2048]{1,0:T(8,128)(2,1)S(1)} %dynamic_slice.25), channel_id=1, source_target_pairs={{0,4},{4,8},{8,12},{12,16},{16,20},{20,24},{24,28},{28,32},{32,36}... | collective-permute-start | bytes 393224 | tf_op jit(solution)/shard_map/ppermute | solution.py:46
  16.2 16.1 %collective-permute-start = (bf16[64,1024]{1,0:T(8,128)(2,1)S(1)}, bf16[64,1024]{1,0:T(8,128)(2,1)S(1)}, u32[]{:S(2)}, u32[]{:S(2)}) collective-permute-start(bf16[64,1024]{1,0:T(8,128)(2,1)S(1)} %get-tuple-element.80), channel_id=1, source_target_pairs={{0,16},{1,49},{16,32},{17,1},{32,48},{33,17},{48,0},{49,33},{2,18}... | collective-permute-start | bytes 393224 | tf_op jit(solution)/shard_map/ppermute | solution.py:29
  17.7 14.6 %collective-permute-start.1 = (bf16[64,1024]{1,0:T(8,128)(2,1)S(1)}, bf16[64,1024]{1,0:T(8,128)(2,1)S(1)}, u32[]{:S(2)}, u32[]{:S(2)}) collective-permute-start(bf16[64,1024]{1,0:T(8,128)(2,1)S(1)} %get-tuple-element.81), channel_id=1, source_target_pairs={{0,48},{1,17},{16,0},{17,33},{32,16},{33,49},{48,32},{49,1},{2,50}... | collective-permute-start | bytes 393224 | tf_op jit(solution)/shard_map/ppermute | solution.py:29
  19.5 12.9 %collective-permute-start.2 = (bf16[64,1024]{1,0:T(8,128)(2,1)S(1)}, bf16[64,1024]{1,0:T(8,128)(2,1)S(1)}, u32[]{:S(2)}, u32[]{:S(2)}) collective-permute-start(bf16[64,1024]{1,0:T(8,128)(2,1)S(1)} %get-tuple-element.82), channel_id=1, source_target_pairs={{0,32},{1,33},{16,48},{17,49},{32,0},{33,1},{48,16},{49,17},{2,34}... | collective-permute-start | bytes 393224 | tf_op jit(solution)/shard_map/ppermute | solution.py:29
  24.0 8.3 %collective-permute-start.4 = (f32[8,128]{1,0:T(8,128)}, f32[8,128]{1,0:T(8,128)S(1)}, u32[]{:S(2)}, u32[]{:S(2)}) collective-permute-start(f32[8,128]{1,0:T(8,128)} %get-tuple-element.84), channel_id=1, source_target_pairs={{0,4},{4,8},{8,12},{12,16},{16,20},{20,24},{24,28},{28,32},{32,36}... | collective-permute-start | bytes 12296 | tf_op jit(solution)/shard_map/ppermute | solution.py:46
  36.0 10.6 %collective-permute-start.5 = (bf16[4,64,512]{2,1,0:T(8,128)(2,1)S(1)}, bf16[4,64,512]{2,1,0:T(8,128)(2,1)S(1)}, u32[]{:S(2)}, u32[]{:S(2)}) collective-permute-start(bf16[4,64,512]{2,1,0:T(8,128)(2,1)S(1)} %get-tuple-element.153), channel_id=1, source_target_pairs={{0,4},{1,13},{4,8},{5,1},{8,12},{9,5},{12,0},{13,9},{2,6},{3,15},{... | collective-permute-start | bytes 786440 | tf_op jit(solution)/shard_map/ppermute | solution.py:29
  38.8 10.4 %collective-permute-start.6 = (bf16[4,64,512]{2,1,0:T(8,128)(2,1)S(1)}, bf16[4,64,512]{2,1,0:T(8,128)(2,1)S(1)}, u32[]{:S(2)}, u32[]{:S(2)}) collective-permute-start(bf16[4,64,512]{2,1,0:T(8,128)(2,1)S(1)} %get-tuple-element.153), channel_id=1, source_target_pairs={{0,12},{1,5},{4,0},{5,9},{8,4},{9,13},{12,8},{13,1},{2,14},{3,7},{... | collective-permute-start | bytes 786440 | tf_op jit(solution)/shard_map/ppermute | solution.py:29
  49.3 10.9 %collective-permute-start.7 = (bf16[4,64,512]{2,1,0:T(8,128)(2,1)S(1)}, bf16[4,64,512]{2,1,0:T(8,128)(2,1)S(1)}, u32[]{:S(2)}, u32[]{:S(2)}) collective-permute-start(bf16[4,64,512]{2,1,0:T(8,128)(2,1)S(1)} %collective-permute-done.5), channel_id=1, source_target_pairs={{0,4},{1,13},{4,8},{5,1},{8,12},{9,5},{12,0},{13,9},{2,6},{3,15},{... | collective-permute-start | bytes 786440 | tf_op jit(solution)/shard_map/ppermute | solution.py:29
  60.4 22.9 %collective-permute-start.8 = (bf16[4,4,64,512]{3,2,1,0:T(8,128)(2,1)S(1)}, bf16[4,4,64,512]{3,2,1,0:T(8,128)(2,1)}, u32[]{:S(2)}, u32[]{:S(2)}) collective-permute-start(bf16[4,4,64,512]{3,2,1,0:T(8,128)(2,1)S(1)} %pad_maximum_fusion.refs_0_), channel_id=1, source_target_pairs={{0,64},{1,193},{64,128},{65,1},{128,192},{129,65},{192,0},{193,129... | collective-permute-start | bytes 3145736 | tf_op jit(solution)/shard_map/ppermute | solution.py:29
  64.1 19.2 %collective-permute-start.9 = (bf16[4,4,64,512]{3,2,1,0:T(8,128)(2,1)S(1)}, bf16[4,4,64,512]{3,2,1,0:T(8,128)(2,1)S(1)}, u32[]{:S(2)}, u32[]{:S(2)}) collective-permute-start(bf16[4,4,64,512]{3,2,1,0:T(8,128)(2,1)S(1)} %pad_maximum_fusion.refs_0_), channel_id=1, source_target_pairs={{0,192},{1,65},{64,0},{65,129},{128,64},{129,193},{192,128},{193,1... | collective-permute-start | bytes 3145736 | tf_op jit(solution)/shard_map/ppermute | solution.py:29
  66.8 12.1 %collective-permute-start.10 = (bf16[4,64,512]{2,1,0:T(8,128)(2,1)S(1)}, bf16[4,64,512]{2,1,0:T(8,128)(2,1)S(1)}, u32[]{:S(2)}, u32[]{:S(2)}) collective-permute-start(bf16[4,64,512]{2,1,0:T(8,128)(2,1)S(1)} %get-tuple-element.94), channel_id=1, source_target_pairs={{0,4},{1,13},{4,8},{5,1},{8,12},{9,5},{12,0},{13,9},{2,6},{3,15},{... | collective-permute-start | bytes 786440 | tf_op jit(solution)/shard_map/ppermute | solution.py:29
  68.3 10.7 %collective-permute-start.11 = (bf16[4,64,512]{2,1,0:T(8,128)(2,1)S(1)}, bf16[4,64,512]{2,1,0:T(8,128)(2,1)S(1)}, u32[]{:S(2)}, u32[]{:S(2)}) collective-permute-start(bf16[4,64,512]{2,1,0:T(8,128)(2,1)S(1)} %get-tuple-element.94), channel_id=1, source_target_pairs={{0,12},{1,5},{4,0},{5,9},{8,4},{9,13},{12,8},{13,1},{2,14},{3,7},{... | collective-permute-start | bytes 786440 | tf_op jit(solution)/shard_map/ppermute | solution.py:29
  83.3 18.7 %collective-permute-start.13 = (bf16[4,4,64,512]{3,2,1,0:T(8,128)(2,1)}, bf16[4,4,64,512]{3,2,1,0:T(8,128)(2,1)}, u32[]{:S(2)}, u32[]{:S(2)}) collective-permute-start(bf16[4,4,64,512]{3,2,1,0:T(8,128)(2,1)} %collective-permute-done.8.refs_1_), channel_id=1, source_target_pairs={{0,64},{1,193},{64,128},{65,1},{128,192},{129,65},{192,0},{193,129... | collective-permute-start | bytes 3145736 | tf_op jit(solution)/shard_map/ppermute | solution.py:29
  84.2 16.6 %collective-permute-start.12 = (bf16[4,64,512]{2,1,0:T(8,128)(2,1)S(1)}, bf16[4,64,512]{2,1,0:T(8,128)(2,1)}, u32[]{:S(2)}, u32[]{:S(2)}) collective-permute-start(bf16[4,64,512]{2,1,0:T(8,128)(2,1)S(1)} %collective-permute-done.10), channel_id=1, source_target_pairs={{0,4},{1,13},{4,8},{5,1},{8,12},{9,5},{12,0},{13,9},{2,6},{3,15},{... | collective-permute-start | bytes 786440 | tf_op jit(solution)/shard_map/ppermute | solution.py:29
  102.0 20.1 %collective-permute-start.14 = (bf16[4,4,64,512]{3,2,1,0:T(8,128)(2,1)S(1)}, bf16[4,4,64,512]{3,2,1,0:T(8,128)(2,1)}, u32[]{:S(2)}, u32[]{:S(2)}) collective-permute-start(bf16[4,4,64,512]{3,2,1,0:T(8,128)(2,1)S(1)} %pad_maximum_fusion.1.refs_0_), channel_id=1, source_target_pairs={{0,64},{1,193},{64,128},{65,1},{128,192},{129,65},{192,0},{193,129... | collective-permute-start | bytes 3145736 | tf_op jit(solution)/shard_map/ppermute | solution.py:29
  103.3 18.8 %collective-permute-start.15 = (bf16[4,4,64,512]{3,2,1,0:T(8,128)(2,1)S(1)}, bf16[4,4,64,512]{3,2,1,0:T(8,128)(2,1)S(1)}, u32[]{:S(2)}, u32[]{:S(2)}) collective-permute-start(bf16[4,4,64,512]{3,2,1,0:T(8,128)(2,1)S(1)} %pad_maximum_fusion.1.refs_0_), channel_id=1, source_target_pairs={{0,192},{1,65},{64,0},{65,129},{128,64},{129,193},{192,128},{193,1... | collective-permute-start | bytes 3145736 | tf_op jit(solution)/shard_map/ppermute | solution.py:29
  123.1 17.7 %collective-permute-start.16 = (bf16[4,4,64,512]{3,2,1,0:T(8,128)(2,1)}, bf16[4,4,64,512]{3,2,1,0:T(8,128)(2,1)S(1)}, u32[]{:S(2)}, u32[]{:S(2)}) collective-permute-start(bf16[4,4,64,512]{3,2,1,0:T(8,128)(2,1)} %collective-permute-done.14.refs_1_), channel_id=1, source_target_pairs={{0,64},{1,193},{64,128},{65,1},{128,192},{129,65},{192,0},{193,129... | collective-permute-start | bytes 3145736 | tf_op jit(solution)/shard_map/ppermute | solution.py:29
  123.1 27.8 %collective-permute-start.17 = (f32[256,512]{1,0:T(8,128)}, f32[256,512]{1,0:T(8,128)S(1)}, u32[]{:S(2)}, u32[]{:S(2)}) collective-permute-start(f32[256,512]{1,0:T(8,128)} %get-tuple-element.120), channel_id=1, source_target_pairs={{0,16},{1,49},{16,32},{17,1},{32,48},{33,17},{48,0},{49,33},{2,18}... | collective-permute-start | bytes 1572872 | tf_op jit(solution)/shard_map/ppermute | solution.py:29
  125.4 25.4 %collective-permute-start.18 = (f32[256,512]{1,0:T(8,128)}, f32[256,512]{1,0:T(8,128)S(1)}, u32[]{:S(2)}, u32[]{:S(2)}) collective-permute-start(f32[256,512]{1,0:T(8,128)} %get-tuple-element.121), channel_id=1, source_target_pairs={{0,48},{1,17},{16,0},{17,33},{32,16},{33,49},{48,32},{49,1},{2,50}... | collective-permute-start | bytes 1572872 | tf_op jit(solution)/shard_map/ppermute | solution.py:29
  127.4 28.4 %collective-permute-start.19 = (f32[256,512]{1,0:T(8,128)}, f32[256,512]{1,0:T(8,128)S(1)}, u32[]{:S(2)}, u32[]{:S(2)}) collective-permute-start(f32[256,512]{1,0:T(8,128)} %get-tuple-element.122), channel_id=1, source_target_pairs={{0,32},{1,33},{16,48},{17,49},{32,0},{33,1},{48,16},{49,17},{2,34}... | collective-permute-start | bytes 1572872 | tf_op jit(solution)/shard_map/ppermute | solution.py:29
  132.0 18.9 %collective-permute-start.20 = (bf16[2,32,3712]{2,1,0:T(8,128)(2,1)S(1)}, bf16[2,32,3712]{2,1,0:T(8,128)(2,1)S(1)}, u32[]{:S(2)}, u32[]{:S(2)}) collective-permute-start(bf16[2,32,3712]{2,1,0:T(8,128)(2,1)S(1)} %pad_maximum_fusion.3), channel_id=1, source_target_pairs={{0,4},{4,8},{8,12},{12,16},{16,20},{20,24},{24,28},{28,32},{32,36}... | collective-permute-start | bytes 1425416 | tf_op jit(solution)/shard_map/ppermute | solution.py:46
  155.8 21.3 %collective-permute-start.21 = (f32[256,512]{1,0:T(8,128)}, f32[256,512]{1,0:T(8,128)S(1)}, u32[]{:S(2)}, u32[]{:S(2)}) collective-permute-start(f32[256,512]{1,0:T(8,128)} %get-tuple-element.129), channel_id=1, source_target_pairs={{0,16},{1,49},{16,32},{17,1},{32,48},{33,17},{48,0},{49,33},{2,18}... | collective-permute-start | bytes 1572872 | tf_op jit(solution)/shard_map/ppermute | solution.py:29
  155.8 21.3 %collective-permute-start.22 = (f32[256,512]{1,0:T(8,128)}, f32[256,512]{1,0:T(8,128)S(1)}, u32[]{:S(2)}, u32[]{:S(2)}) collective-permute-start(f32[256,512]{1,0:T(8,128)} %get-tuple-element.130), channel_id=1, source_target_pairs={{0,48},{1,17},{16,0},{17,33},{32,16},{33,49},{48,32},{49,1},{2,50}... | collective-permute-start | bytes 1572872 | tf_op jit(solution)/shard_map/ppermute | solution.py:29
  159.0 18.1 %collective-permute-start.23 = (f32[256,512]{1,0:T(8,128)}, f32[256,512]{1,0:T(8,128)S(1)}, u32[]{:S(2)}, u32[]{:S(2)}) collective-permute-start(f32[256,512]{1,0:T(8,128)} %get-tuple-element.140), channel_id=1, source_target_pairs={{0,32},{1,33},{16,48},{17,49},{32,0},{33,1},{48,16},{49,17},{2,34}... | collective-permute-start | bytes 1572872 | tf_op jit(solution)/shard_map/ppermute | solution.py:29
  204.3 13.7 %collective-permute-start.24 = (f32[1,128]{1,0:T(1,128)}, f32[1,128]{1,0:T(1,128)S(1)}, u32[]{:S(2)}, u32[]{:S(2)}) collective-permute-start(f32[1,128]{1,0:T(1,128)} %get-tuple-element.144), channel_id=1, source_target_pairs={{0,4},{4,0},{8,12},{12,8},{1,5},{5,1},{9,13},{13,9},{2,6},{6,2},{1... | collective-permute-start | bytes 1544 | tf_op jit(solution)/shard_map/ppermute | solution.py:34
  204.3 13.7 %collective-permute-start.25 = (f32[1,128]{1,0:T(1,128)}, f32[1,128]{1,0:T(1,128)S(1)}, u32[]{:S(2)}, u32[]{:S(2)}) collective-permute-start(f32[1,128]{1,0:T(1,128)} %get-tuple-element.144), channel_id=1, source_target_pairs={{0,8},{4,12},{8,0},{12,4},{1,9},{5,13},{9,1},{13,5},{2,10},{6,14},... | collective-permute-start | bytes 1544 | tf_op jit(solution)/shard_map/ppermute | solution.py:34
  204.3 13.7 %collective-permute-start.26 = (f32[1,128]{1,0:T(1,128)}, f32[1,128]{1,0:T(1,128)S(1)}, u32[]{:S(2)}, u32[]{:S(2)}) collective-permute-start(f32[1,128]{1,0:T(1,128)} %get-tuple-element.144), channel_id=1, source_target_pairs={{0,12},{4,8},{8,4},{12,0},{1,13},{5,9},{9,5},{13,1},{2,14},{6,10},... | collective-permute-start | bytes 1544 | tf_op jit(solution)/shard_map/ppermute | solution.py:34
  218.1 4.8 %collective-permute-start.27 = (f32[1,128]{1,0:T(1,128)S(1)}, f32[1,128]{1,0:T(1,128)S(1)}, u32[]{:S(2)}, u32[]{:S(2)}) collective-permute-start(f32[1,128]{1,0:T(1,128)S(1)} %add_add_fusion.1), channel_id=1, source_target_pairs={{0,64},{64,0},{128,192},{192,128},{1,65},{65,1},{129,193},{193,129... | collective-permute-start | bytes 1544 | tf_op jit(solution)/shard_map/ppermute | solution.py:34
  219.9 5.0 %collective-permute-start.28 = (f32[1,128]{1,0:T(1,128)S(1)}, f32[1,128]{1,0:T(1,128)S(1)}, u32[]{:S(2)}, u32[]{:S(2)}) collective-permute-start(f32[1,128]{1,0:T(1,128)S(1)} %add_add_fusion.1), channel_id=1, source_target_pairs={{0,128},{64,192},{128,0},{192,64},{1,129},{65,193},{129,1},{193,65... | collective-permute-start | bytes 1544 | tf_op jit(solution)/shard_map/ppermute | solution.py:34
  221.4 4.8 %collective-permute-start.29 = (f32[1,128]{1,0:T(1,128)S(1)}, f32[1,128]{1,0:T(1,128)S(1)}, u32[]{:S(2)}, u32[]{:S(2)}) collective-permute-start(f32[1,128]{1,0:T(1,128)S(1)} %add_add_fusion.1), channel_id=1, source_target_pairs={{0,192},{64,128},{128,64},{192,0},{1,193},{65,129},{129,65},{193,1... | collective-permute-start | bytes 1544 | tf_op jit(solution)/shard_map/ppermute | solution.py:34
  226.2 5.1 %collective-permute-start.31 = (f32[1,128]{1,0:T(1,128)S(1)}, f32[1,128]{1,0:T(1,128)S(1)}, u32[]{:S(2)}, u32[]{:S(2)}) collective-permute-start(f32[1,128]{1,0:T(1,128)S(1)} %add_add_fusion), channel_id=1, source_target_pairs={{0,32},{16,48},{32,0},{48,16},{1,33},{17,49},{33,1},{49,17},{2,34}... | collective-permute-start | bytes 1544 | tf_op jit(solution)/shard_map/ppermute | solution.py:34
  (18 other events, 172.0 us)
Sparse Core Ops, SparseCore 0:
  35.9 51.7 all-gather.2

commit v3 on v2

--- a/solution.py
+++ b/solution.py
@@ -149,7 +149,7 @@
             pltpu.SemaphoreType.DMA((4, 8)),
         ],
         out_shape=[jax.ShapeDtypeStruct((ROWS, wide), jnp.float32)] * 4,
-        compiler_params=pltpu.CompilerParams(vmem_limit_bytes=60 * MIB),
+        compiler_params=pltpu.CompilerParams(vmem_limit_bytes=28 * MIB),
         cost_estimate=pl.CostEstimate(
             flops=8 * ROWS * D * wide, bytes_accessed=2 * D * (1024 + wide), transcendentals=0
         ),
@@ -195,7 +195,7 @@
             out_specs=pl.BlockSpec((1, 1, LANES), lambda i, pos: (i, 0, 0)),
         ),
         out_shape=jax.ShapeDtypeStruct((2, 1, LANES), jnp.float32),
-        compiler_params=pltpu.CompilerParams(vmem_limit_bytes=60 * MIB),
+        compiler_params=pltpu.CompilerParams(vmem_limit_bytes=40 * MIB),
         cost_estimate=pl.CostEstimate(
             flops=8 * ROWS * MINE, bytes_accessed=8 * ROWS * MINE, transcendentals=ROWS * MINE
         ),
@@ -303,14 +303,12 @@
     chunks = [lax.dynamic_slice_in_dim(columns, x * STEP, CHUNK, 1) for x in to_x]
     chunks, target_rows, kept, lengths = tie(chunks, target_rows, kept, lengths)
     sent = [chunks[0]] + [swing(chunks[way], "x", way) for way in (SIDE, OTHER, FAR)]
-    count = jnp.full((1, LANES), jnp.sum(lengths).astype(jnp.float32))
+    sent, target_rows, lengths, kept = tie(sent, target_rows, lengths, kept)
     tail = onward(lax.dynamic_slice(target_rows, (kept, at["c"] * 2048), (SPARE, 2048)))
     nums = jnp.stack([lengths[0], lengths[1], kept]).astype(jnp.int32)
     info, info_tail = infos(nums, advantages, old_logp.reshape(1, ROWS))
     info_tail = onward(info_tail)
-    sent, lengths, kept, count, tail, info_tail = tie(
-        sent, lengths, kept, count, tail, info_tail
-    )
+    count = jnp.full((1, LANES), jnp.sum(lengths).astype(jnp.float32))
     mine = []
     for x in range(4):
         piece = sent[0]
@@ -337,7 +335,7 @@
         return home
 
     side, other = there(block[0], "h")
-    side, other = tie(side, other)
+    side, other, tail = tie(side, other, tail)
     far = again(side, "h")
     where = jnp.stack([kept, at["c"]]).astype(jnp.int32)
     group = lax.all_gather(half_rows(where, target_rows, tail), ("x", "c"), axis=0)
@@ -352,8 +350,8 @@
         if i == 0:
             count = lax.psum(count, "x")
         product = probes(pos, group, parts) if i else None
-        a, b, side, other, count, product, home, tails = tie(
-            a, b, side, other, count, product, home, tails
+        a, b, side, other, count, product, home, tails, info_tail = tie(
+            a, b, side, other, count, product, home, tails, info_tail
         )
         if i:
             home = home + returned(product)

time: 245 us -> 242 us (0.988)
  starting transfers between devices: 69.6 us -> 81.8 us
  blocking collectives: 51.5 us -> 39.8 us
  Pallas kernels: 39.5 us -> 34.1 us
  local copies, waits for them, and re-layouts: 10.7 us -> 14 us
    ppermute x3, starting transfers between devices: 11.1 us -> 22.8 us  [onward(): return lax.ppermute(tail, FS, [(i, i + 1) for i in range(63)])]
    psum x1, blocking collectives: 15.8 us -> 9.09 us  [shards(): count = lax.psum(count, 'h')]
    psum x1, blocking collectives: 18.7 us -> 12.9 us  [shards(): score = lax.psum(scores(pos, gate, up, home), ('l', 'c'))]
    ppermute x3, waiting for transfers between devices: 0.01 us -> 4.72 us  [onward(): return lax.ppermute(tail, FS, [(i, i + 1) for i in range(63)])]
    unnamed x32 -> x40, local copies, waits for them, and re-layouts: 5.34 us -> 10 us
    ppermute x21, waiting for transfers between devices: 41.9 us -> 38.1 us  [swing(): return lax.ppermute(value, (axis, 'c'), pairs)]
    ppermute x9, starting transfers between devices: 16 us -> 19.4 us  [mix(): return lax.ppermute(value, axis, [(i, i ^ bit) for i in range(n)])]
    pallas_call x2, Pallas kernels: 18 us -> 14.7 us  [probes(): pl.pallas_call(probe_kernel, in_specs=[pl.BlockSpec(memory_space=pltpu.SM...]
  transfers between devices with their start and end apart: 34 -> 34, of which waited for: 13 -> 13; matrix products, arithmetic and copies ran while one was open for 2% -> 2% of each run, Pallas kernels for 13% -> 11%
where the time goes in v3:
time: 242 us; the launch traced here: 240 us
  starting transfers between devices  81.8 us (34%)
  waiting for transfers between devices  48 us (20%)
  blocking collectives  39.8 us (16%)
  Pallas kernels  34.1 us (14%)
  between operations  18.9 us (8%)
  local copies, waits for them, and re-layouts  14 us (6%)
  other arithmetic  3.37 us (1%)
    ppermute x21, starting transfers between devices, swing(): return lax.ppermute(value, (axis, 'c'), pairs)  39.5 us
    ppermute x21, waiting for transfers between devices, swing(): return lax.ppermute(value, (axis, 'c'), pairs)  38.1 us
    ppermute x3, starting transfers between devices, onward(): return lax.ppermute(tail, FS, [(i, i + 1) for i in range(63)])  22.8 us
    ppermute x9, starting transfers between devices, mix(): return lax.ppermute(value, axis, [(i, i ^ bit) for i in range(n)])  19.4 us
    pallas_call x2, Pallas kernels, probes(): pl.pallas_call(probe_kernel, in_specs=[pl.BlockSpec(memory_space=pltpu.SM...  14.7 us
    psum x1, blocking collectives, shards(): score = lax.psum(scores(pos, gate, up, home), ('l', 'c'))  12.9 us
    unnamed x40, local copies, waits for them, and re-layouts  10 us
    psum x1, blocking collectives, shards(): count = lax.psum(count, 'x')  9.43 us
  transfers between devices with their start and end apart: 34, of which 13 were waited for; matrix products, arithmetic and copies ran while one was open for 2% of the time, Pallas kernels for 11%

profile of v3, /device:TPU:0, one launch (start us, length us, event | category | flops | bytes accessed | tf_op | source)
XLA Modules:
  0.0 240.1 jit_solution(14951815464635558554)
XLA Ops:
  11.8 3.2 %collective-permute-start.1 = (bf16[64,1024]{1,0:T(8,128)(2,1)S(1)}, bf16[64,1024]{1,0:T(8,128)(2,1)S(1)}, u32[]{:S(2)}, u32[]{:S(2)}) collective-permute-start(bf16[64,1024]{1,0:T(8,128)(2,1)S(1)} %get-tuple-element.81), channel_id=1, source_target_pairs={{0,48},{1,17},{16,0},{17,33},{32,16},{33,49},{48,32},{49,1},{2,50}... | collective-permute-start | bytes 393224 | tf_op jit(solution)/shard_map/ppermute | solution.py:29
  15.1 6.7 %collective-permute-done = bf16[64,1024]{1,0:T(8,128)(2,1)S(1)} collective-permute-done((bf16[64,1024]{1,0:T(8,128)(2,1)S(1)}, bf16[64,1024]{1,0:T(8,128)(2,1)S(1)}, u32[]{:S(2)}, u32[]{:S(2)}) %collective-permute-start) | collective-permute-done | bytes 131104 | tf_op jit(solution)/shard_map/ppermute | solution.py:29
  24.4 3.1 %collective-permute-start.4 = (bf16[4,64,512]{2,1,0:T(8,128)(2,1)S(1)}, bf16[4,64,512]{2,1,0:T(8,128)(2,1)S(1)}, u32[]{:S(2)}, u32[]{:S(2)}) collective-permute-start(bf16[4,64,512]{2,1,0:T(8,128)(2,1)S(1)} %get-tuple-element.157), channel_id=1, source_target_pairs={{0,12},{1,5},{4,0},{5,9},{8,4},{9,13},{12,8},{13,1},{2,14},{3,7},{... | collective-permute-start | bytes 786440 | tf_op jit(solution)/shard_map/ppermute | solution.py:29
  27.6 3.3 %collective-permute-start.5 = (bf16[32,2048]{1,0:T(8,128)(2,1)S(1)}, bf16[32,2048]{1,0:T(8,128)(2,1)S(1)}, u32[]{:S(2)}, u32[]{:S(2)}) collective-permute-start(bf16[32,2048]{1,0:T(8,128)(2,1)S(1)} %dynamic_slice.25), channel_id=1, source_target_pairs={{0,4},{4,8},{8,12},{12,16},{16,20},{20,24},{24,28},{28,32},{32,36}... | collective-permute-start | bytes 393224 | tf_op jit(solution)/shard_map/ppermute | solution.py:46
  31.0 4.7 %collective-permute-done.5.tail = bf16[32,2048]{1,0:T(8,128)(2,1)S(1)} collective-permute-done((bf16[32,2048]{1,0:T(8,128)(2,1)S(1)}, bf16[32,2048]{1,0:T(8,128)(2,1)S(1)}, u32[]{:S(2)}, u32[]{:S(2)}) %collective-permute-start.5) | collective-permute-done | bytes 131104 | tf_op jit(solution)/shard_map/ppermute | solution.py:46
  35.7 2.6 %collective-permute-done.4 = bf16[4,64,512]{2,1,0:T(8,128)(2,1)S(1)} collective-permute-done((bf16[4,64,512]{2,1,0:T(8,128)(2,1)S(1)}, bf16[4,64,512]{2,1,0:T(8,128)(2,1)S(1)}, u32[]{:S(2)}, u32[]{:S(2)}) %collective-permute-start.4) | collective-permute-done | bytes 262176 | tf_op jit(solution)/shard_map/ppermute | solution.py:29
  40.1 7.2 %collective-permute-start.6 = (bf16[4,64,512]{2,1,0:T(8,128)(2,1)S(1)}, bf16[4,64,512]{2,1,0:T(8,128)(2,1)S(1)}, u32[]{:S(2)}, u32[]{:S(2)}) collective-permute-start(bf16[4,64,512]{2,1,0:T(8,128)(2,1)S(1)} %collective-permute-done.3), channel_id=1, source_target_pairs={{0,4},{1,13},{4,8},{5,1},{8,12},{9,5},{12,0},{13,9},{2,6},{3,15},{... | collective-permute-start | bytes 786440 | tf_op jit(solution)/shard_map/ppermute | solution.py:29
  48.6 6.9 %collective-permute-done.6 = bf16[4,64,512]{2,1,0:T(8,128)(2,1)S(1)} collective-permute-done((bf16[4,64,512]{2,1,0:T(8,128)(2,1)S(1)}, bf16[4,64,512]{2,1,0:T(8,128)(2,1)S(1)}, u32[]{:S(2)}, u32[]{:S(2)}) %collective-permute-start.6) | collective-permute-done | bytes 262176 | tf_op jit(solution)/shard_map/ppermute | solution.py:29
  60.9 4.8 %collective-permute-start.11 = (f32[8,128]{1,0:T(8,128)}, f32[8,128]{1,0:T(8,128)S(1)}, u32[]{:S(2)}, u32[]{:S(2)}) collective-permute-start(f32[8,128]{1,0:T(8,128)} %get-tuple-element.99), channel_id=1, source_target_pairs={{0,4},{4,8},{8,12},{12,16},{16,20},{20,24},{24,28},{28,32},{32,36}... | collective-permute-start | bytes 12296 | tf_op jit(solution)/shard_map/ppermute | solution.py:46
  71.8 9.4 %psum.28 = f32[1,128]{1,0:T(1,128)S(1)} all-reduce(f32[1,128]{1,0:T(1,128)S(1)} %broadcast_in_dim.3), channel_id=1, replica_groups=mesh['y'=4,'x'=4,'h'=4,'l'=2,'c'=2] {'x'}, use_global_device_ids=true, to_apply=%region_1.2 | all-reduce | flops 128 | bytes 1024 | tf_op jit(solution)/shard_map/psum | solution.py:351
  82.6 4.0 %collective-permute-start.12 = (bf16[4,64,512]{2,1,0:T(8,128)(2,1)S(1)}, bf16[4,64,512]{2,1,0:T(8,128)(2,1)}, u32[]{:S(2)}, u32[]{:S(2)}) collective-permute-start(bf16[4,64,512]{2,1,0:T(8,128)(2,1)S(1)} %collective-permute-done.9), channel_id=1, source_target_pairs={{0,4},{1,13},{4,8},{5,1},{8,12},{9,5},{12,0},{13,9},{2,6},{3,15},{... | collective-permute-start | bytes 786440 | tf_op jit(solution)/shard_map/ppermute | solution.py:29
  86.7 9.1 %psum.29 = f32[1,128]{1,0:T(1,128)S(1)} all-reduce(f32[1,128]{1,0:T(1,128)S(1)} %psum.28), channel_id=1, replica_groups=mesh['y'=4,'x'=4,'h'=4,'l'=2,'c'=2] {'h'}, use_global_device_ids=true, to_apply=%region_2.3 | all-reduce | flops 128 | bytes 1024 | tf_op jit(solution)/shard_map/psum | solution.py:362
  96.9 5.5 %collective-permute-done.13.refs_3_ = bf16[4,4,64,512]{3,2,1,0:T(8,128)(2,1)} collective-permute-done((bf16[4,4,64,512]{3,2,1,0:T(8,128)(2,1)}, bf16[4,4,64,512]{3,2,1,0:T(8,128)(2,1)}, u32[]{:S(2)}, u32[]{:S(2)}) %collective-permute-start.13) | collective-permute-done | bytes 1048608 | tf_op jit(solution)/shard_map/ppermute | solution.py:29
  102.3 3.2 %collective-permute-start.15 = (bf16[4,4,64,512]{3,2,1,0:T(8,128)(2,1)S(1)}, bf16[4,4,64,512]{3,2,1,0:T(8,128)(2,1)}, u32[]{:S(2)}, u32[]{:S(2)}) collective-permute-start(bf16[4,4,64,512]{3,2,1,0:T(8,128)(2,1)S(1)} %pad_maximum_fusion.1.refs_0_), channel_id=1, source_target_pairs={{0,192},{1,65},{64,0},{65,129},{128,64},{129,193},{192,128},{193,1... | collective-permute-start | bytes 3145736 | tf_op jit(solution)/shard_map/ppermute | solution.py:29
  105.7 3.4 %copy-done.12 = bf16[2048,2048]{1,0:T(8,128)(2,1)S(1)} copy-done((bf16[2048,2048]{1,0:T(8,128)(2,1)S(1)}, bf16[2048,2048]{1,0:T(8,128)(2,1)}, u32[]{:S(2)}) %copy-start.12) | copy-done | bytes 8388632
  110.3 6.8 %probe.2 = (f32[256,512]{1,0:T(8,128)S(1)}, f32[256,512]{1,0:T(8,128)S(1)}, f32[256,512]{1,0:T(8,128)S(1)}, f32[256,512]{1,0:T(8,128)S(1)}) custom-call(s32[12]{0:T(128)S(1)} %stack.120.pos, bf16[8,256,2048]{2,1,0:T(8,128)(2,1)S(1)} %bitcast.48, bf16[4,4,64,512]{3,2,1,0:T(8,128)(2,1)S(1)} %pad_maximum_fusion.refs_0_, ...), custom_call_target="tpu_custom_call" | custom-call | flops 4294967296 | bytes 12582912 | tf_op jit(solution)/shard_map/probe/pallas_call | solution.py:142
  117.2 3.9 %collective-permute-done.14.refs_1_ = bf16[4,4,64,512]{3,2,1,0:T(8,128)(2,1)} collective-permute-done((bf16[4,4,64,512]{3,2,1,0:T(8,128)(2,1)S(1)}, bf16[4,4,64,512]{3,2,1,0:T(8,128)(2,1)}, u32[]{:S(2)}, u32[]{:S(2)}) %collective-permute-start.14) | collective-permute-done | bytes 1048608 | tf_op jit(solution)/shard_map/ppermute | solution.py:29
  123.9 3.2 %collective-permute-start.18 = (f32[256,512]{1,0:T(8,128)S(1)}, f32[256,512]{1,0:T(8,128)S(1)}, u32[]{:S(2)}, u32[]{:S(2)}) collective-permute-start(f32[256,512]{1,0:T(8,128)S(1)} %get-tuple-element.125), channel_id=1, source_target_pairs={{0,48},{1,17},{16,0},{17,33},{32,16},{33,49},{48,32},{49,1},{2,50}... | collective-permute-start | bytes 1572872 | tf_op jit(solution)/shard_map/ppermute | solution.py:29
  127.2 14.7 %collective-permute-start.20 = (bf16[2,32,3712]{2,1,0:T(8,128)(2,1)S(1)}, bf16[2,32,3712]{2,1,0:T(8,128)(2,1)S(1)}, u32[]{:S(2)}, u32[]{:S(2)}) collective-permute-start(bf16[2,32,3712]{2,1,0:T(8,128)(2,1)S(1)} %pad_maximum_fusion.3), channel_id=1, source_target_pairs={{0,4},{4,8},{8,12},{12,16},{16,20},{20,24},{24,28},{28,32},{32,36}... | collective-permute-start | bytes 1425416 | tf_op jit(solution)/shard_map/ppermute | solution.py:46
  144.7 7.9 %probe.3 = (f32[256,512]{1,0:T(8,128)S(1)}, f32[256,512]{1,0:T(8,128)}, f32[256,512]{1,0:T(8,128)}, f32[256,512]{1,0:T(8,128)}) custom-call(s32[12]{0:T(128)S(1)} %stack.120.pos, bf16[8,256,2048]{2,1,0:T(8,128)(2,1)S(1)} %bitcast.49, bf16[4,4,64,512]{3,2,1,0:T(8,128)(2,1)S(1)} %copy-done.10, bf16[4,4,64,512]{3,2,1,0:T(8,128)(2,1)} %collective-permute-done.14.refs_1_, ...), custom_call_target="tpu_custom_call" | custom-call | flops 4294967296 | bytes 12582912 | tf_op jit(solution)/shard_map/probe/pallas_call | solution.py:142
  152.6 5.3 %collective-permute-done.17.refs_1_ = f32[256,512]{1,0:T(8,128)S(1)} collective-permute-done((f32[256,512]{1,0:T(8,128)S(1)}, f32[256,512]{1,0:T(8,128)S(1)}, u32[]{:S(2)}, u32[]{:S(2)}) %collective-permute-start.17) | collective-permute-done | bytes 524320 | tf_op jit(solution)/shard_map/ppermute | solution.py:29
  158.1 3.2 %collective-permute-start.22 = (f32[256,512]{1,0:T(8,128)}, f32[256,512]{1,0:T(8,128)}, u32[]{:S(2)}, u32[]{:S(2)}) collective-permute-start(f32[256,512]{1,0:T(8,128)} %get-tuple-element.134), channel_id=1, source_target_pairs={{0,48},{1,17},{16,0},{17,33},{32,16},{33,49},{48,32},{49,1},{2,50}... | collective-permute-start | bytes 1572872 | tf_op jit(solution)/shard_map/ppermute | solution.py:29
  161.3 4.3 %place.1 = (bf16[256,3712]{1,0:T(8,128)(2,1)}, bf16[256,3712]{1,0:T(8,128)(2,1)}) custom-call(s32[1]{0:T(128)} %bitcast.5.kept, bf16[256,3712]{1,0:T(8,128)(2,1)} %gate.1, bf16[256,3712]{1,0:T(8,128)(2,1)} %up.1, bf16[2,32,3712]{2,1,0:T(8,128)(2,1)} %copy-done.15), custom_call_target="tpu_custom_call" | custom-call | bytes 7602176 | tf_op jit(solution)/shard_map/place/pallas_call | solution.py:95
  165.6 8.4 %psum.30.count_ref = f32[1,128]{1,0:T(1,128)} all-reduce(f32[1,128]{1,0:T(1,128)S(1)} %psum.29), channel_id=1, replica_groups=mesh['y'=4,'x'=4,'h'=4,'l'=2,'c'=2] {'y'}, use_global_device_ids=true, to_apply=%region_3.4 | all-reduce | flops 128 | bytes 1024 | tf_op jit(solution)/shard_map/psum | solution.py:368
  174.0 4.0 %collective-permute-done.21.refs_5_ = f32[256,512]{1,0:T(8,128)S(1)} collective-permute-done((f32[256,512]{1,0:T(8,128)}, f32[256,512]{1,0:T(8,128)S(1)}, u32[]{:S(2)}, u32[]{:S(2)}) %collective-permute-start.21) | collective-permute-done | bytes 524320 | tf_op jit(solution)/shard_map/ppermute | solution.py:29
  181.2 3.1 %score.1 = f32[2,1,128]{2,1,0:T(1,128)S(1)} custom-call(s32[12]{0:T(128)S(1)} %stack.120.pos, bf16[256,3712]{1,0:T(8,128)(2,1)S(1)} %copy-done, bf16[256,3712]{1,0:T(8,128)(2,1)S(1)} %copy-done.1, f32[256,512]{1,0:T(8,128)S(1)} %get-tuple-element.137.refs_0_, f32[256,512]{1,0:T(8,128)S(1)} %collective-permute-done.17.refs_1_, ...), custom_call_target="tpu_custom_call" | custom-call | flops 7602176 | bytes 7602176 | tf_op jit(solution)/shard_map/score/pallas_call | solution.py:189
  184.3 12.9 %psum.31.score_ref = f32[2,1,128]{2,1,0:T(1,128)} all-reduce(f32[2,1,128]{2,1,0:T(1,128)S(1)} %score.1), channel_id=1, replica_groups=mesh['y'=4,'x'=4,'h'=4,'l'=2,'c'=2] {'l','c'}, use_global_device_ids=true, to_apply=%region_4.5 | all-reduce | flops 256 | bytes 2048 | tf_op jit(solution)/shard_map/psum | solution.py:371
  198.9 6.5 %collective-permute-start.26 = (f32[1,128]{1,0:T(1,128)}, f32[1,128]{1,0:T(1,128)S(1)}, u32[]{:S(2)}, u32[]{:S(2)}) collective-permute-start(f32[1,128]{1,0:T(1,128)} %get-tuple-element.148), channel_id=1, source_target_pairs={{0,12},{4,8},{8,4},{12,0},{1,13},{5,9},{9,5},{13,1},{2,14},{6,10},... | collective-permute-start | bytes 1544 | tf_op jit(solution)/shard_map/ppermute | solution.py:34
  205.4 7.2 %grad.1 = (bf16[256,3712]{1,0:T(8,128)(2,1)}, bf16[256,3712]{1,0:T(8,128)(2,1)}) custom-call(s32[12]{0:T(128)} %copy-done.11, bf16[256,3712]{1,0:T(8,128)(2,1)} %get-tuple-element.135.gate_ref, bf16[256,3712]{1,0:T(8,128)(2,1)} %get-tuple-element.136.up_ref, f32[256,128]{1,0:T(8,128)} %get-tuple-element.149.slope_ref, f32[256,512]{1,0:T(8,128)} %copy-done.3, ...), custom_call_target="tpu_custom_call" | custom-call | flops 11403264 | bytes 11403264 | tf_op jit(solution)/shard_map/grad/pallas_call | solution.py:277
  212.7 5.3 %collective-permute-start.27 = (f32[1,128]{1,0:T(1,128)S(1)}, f32[1,128]{1,0:T(1,128)S(1)}, u32[]{:S(2)}, u32[]{:S(2)}) collective-permute-start(f32[1,128]{1,0:T(1,128)S(1)} %add_add_fusion.1), channel_id=1, source_target_pairs={{0,64},{64,0},{128,192},{192,128},{1,65},{65,1},{129,193},{193,129... | collective-permute-start | bytes 1544 | tf_op jit(solution)/shard_map/ppermute | solution.py:34
  218.0 2.8 %collective-permute-start.29 = (f32[1,128]{1,0:T(1,128)S(1)}, f32[1,128]{1,0:T(1,128)S(1)}, u32[]{:S(2)}, u32[]{:S(2)}) collective-permute-start(f32[1,128]{1,0:T(1,128)S(1)} %add_add_fusion.1), channel_id=1, source_target_pairs={{0,192},{64,128},{128,64},{192,0},{1,193},{65,129},{129,65},{193,1... | collective-permute-start | bytes 1544 | tf_op jit(solution)/shard_map/ppermute | solution.py:34
  223.2 2.8 %collective-permute-start.31 = (f32[1,128]{1,0:T(1,128)S(1)}, f32[1,128]{1,0:T(1,128)S(1)}, u32[]{:S(2)}, u32[]{:S(2)}) collective-permute-start(f32[1,128]{1,0:T(1,128)S(1)} %add_add_fusion), channel_id=1, source_target_pairs={{0,32},{16,48},{32,0},{48,16},{1,33},{17,49},{33,1},{49,17},{2,34}... | collective-permute-start | bytes 1544 | tf_op jit(solution)/shard_map/ppermute | solution.py:34
  (107 shorter events, 41.6 us)
Async XLA Ops:
  7.2 98.5 %all-gather.3.cloned.1.call-start = ((), (), s32[]{:S(2)}) async-start(), calls=%async_computation | async-start | bytes 9437184 | tf_op jit(solution)/shard_map/all_gather | solution.py:341
  11.7 10.1 %collective-permute-start = (bf16[64,1024]{1,0:T(8,128)(2,1)S(1)}, bf16[64,1024]{1,0:T(8,128)(2,1)S(1)}, u32[]{:S(2)}, u32[]{:S(2)}) collective-permute-start(bf16[64,1024]{1,0:T(8,128)(2,1)S(1)} %get-tuple-element.80), channel_id=1, source_target_pairs={{0,16},{1,49},{16,32},{17,1},{32,48},{33,17},{48,0},{49,33},{2,18}... | collective-permute-start | bytes 393224 | tf_op jit(solution)/shard_map/ppermute | solution.py:29
  11.8 10.0 %collective-permute-start.1 = (bf16[64,1024]{1,0:T(8,128)(2,1)S(1)}, bf16[64,1024]{1,0:T(8,128)(2,1)S(1)}, u32[]{:S(2)}, u32[]{:S(2)}) collective-permute-start(bf16[64,1024]{1,0:T(8,128)(2,1)S(1)} %get-tuple-element.81), channel_id=1, source_target_pairs={{0,48},{1,17},{16,0},{17,33},{32,16},{33,49},{48,32},{49,1},{2,50}... | collective-permute-start | bytes 393224 | tf_op jit(solution)/shard_map/ppermute | solution.py:29
  15.0 6.8 %collective-permute-start.2 = (bf16[64,1024]{1,0:T(8,128)(2,1)S(1)}, bf16[64,1024]{1,0:T(8,128)(2,1)S(1)}, u32[]{:S(2)}, u32[]{:S(2)}) collective-permute-start(bf16[64,1024]{1,0:T(8,128)(2,1)S(1)} %get-tuple-element.82), channel_id=1, source_target_pairs={{0,32},{1,33},{16,48},{17,49},{32,0},{33,1},{48,16},{49,17},{2,34}... | collective-permute-start | bytes 393224 | tf_op jit(solution)/shard_map/ppermute | solution.py:29
  22.0 13.7 %collective-permute-start.3 = (bf16[4,64,512]{2,1,0:T(8,128)(2,1)S(1)}, bf16[4,64,512]{2,1,0:T(8,128)(2,1)S(1)}, u32[]{:S(2)}, u32[]{:S(2)}) collective-permute-start(bf16[4,64,512]{2,1,0:T(8,128)(2,1)S(1)} %get-tuple-element.157), channel_id=1, source_target_pairs={{0,4},{1,13},{4,8},{5,1},{8,12},{9,5},{12,0},{13,9},{2,6},{3,15},{... | collective-permute-start | bytes 786440 | tf_op jit(solution)/shard_map/ppermute | solution.py:29
  24.4 14.0 %collective-permute-start.4 = (bf16[4,64,512]{2,1,0:T(8,128)(2,1)S(1)}, bf16[4,64,512]{2,1,0:T(8,128)(2,1)S(1)}, u32[]{:S(2)}, u32[]{:S(2)}) collective-permute-start(bf16[4,64,512]{2,1,0:T(8,128)(2,1)S(1)} %get-tuple-element.157), channel_id=1, source_target_pairs={{0,12},{1,5},{4,0},{5,9},{8,4},{9,13},{12,8},{13,1},{2,14},{3,7},{... | collective-permute-start | bytes 786440 | tf_op jit(solution)/shard_map/ppermute | solution.py:29
  27.6 8.1 %collective-permute-start.5 = (bf16[32,2048]{1,0:T(8,128)(2,1)S(1)}, bf16[32,2048]{1,0:T(8,128)(2,1)S(1)}, u32[]{:S(2)}, u32[]{:S(2)}) collective-permute-start(bf16[32,2048]{1,0:T(8,128)(2,1)S(1)} %dynamic_slice.25), channel_id=1, source_target_pairs={{0,4},{4,8},{8,12},{12,16},{16,20},{20,24},{24,28},{28,32},{32,36}... | collective-permute-start | bytes 393224 | tf_op jit(solution)/shard_map/ppermute | solution.py:46
  40.1 15.3 %collective-permute-start.6 = (bf16[4,64,512]{2,1,0:T(8,128)(2,1)S(1)}, bf16[4,64,512]{2,1,0:T(8,128)(2,1)S(1)}, u32[]{:S(2)}, u32[]{:S(2)}) collective-permute-start(bf16[4,64,512]{2,1,0:T(8,128)(2,1)S(1)} %collective-permute-done.3), channel_id=1, source_target_pairs={{0,4},{1,13},{4,8},{5,1},{8,12},{9,5},{12,0},{13,9},{2,6},{3,15},{... | collective-permute-start | bytes 786440 | tf_op jit(solution)/shard_map/ppermute | solution.py:29
  55.6 25.7 %collective-permute-start.7 = (bf16[4,4,64,512]{3,2,1,0:T(8,128)(2,1)S(1)}, bf16[4,4,64,512]{3,2,1,0:T(8,128)(2,1)}, u32[]{:S(2)}, u32[]{:S(2)}) collective-permute-start(bf16[4,4,64,512]{3,2,1,0:T(8,128)(2,1)S(1)} %pad_maximum_fusion.refs_0_), channel_id=1, source_target_pairs={{0,64},{1,193},{64,128},{65,1},{128,192},{129,65},{192,0},{193,129... | collective-permute-start | bytes 3145736 | tf_op jit(solution)/shard_map/ppermute | solution.py:29
  57.2 24.1 %collective-permute-start.8 = (bf16[4,4,64,512]{3,2,1,0:T(8,128)(2,1)S(1)}, bf16[4,4,64,512]{3,2,1,0:T(8,128)(2,1)S(1)}, u32[]{:S(2)}, u32[]{:S(2)}) collective-permute-start(bf16[4,4,64,512]{3,2,1,0:T(8,128)(2,1)S(1)} %pad_maximum_fusion.refs_0_), channel_id=1, source_target_pairs={{0,192},{1,65},{64,0},{65,129},{128,64},{129,193},{192,128},{193,1... | collective-permute-start | bytes 3145736 | tf_op jit(solution)/shard_map/ppermute | solution.py:29
  60.9 20.3 %collective-permute-start.11 = (f32[8,128]{1,0:T(8,128)}, f32[8,128]{1,0:T(8,128)S(1)}, u32[]{:S(2)}, u32[]{:S(2)}) collective-permute-start(f32[8,128]{1,0:T(8,128)} %get-tuple-element.99), channel_id=1, source_target_pairs={{0,4},{4,8},{8,12},{12,16},{16,20},{20,24},{24,28},{28,32},{32,36}... | collective-permute-start | bytes 12296 | tf_op jit(solution)/shard_map/ppermute | solution.py:46
  67.1 14.2 %collective-permute-start.10 = (bf16[4,64,512]{2,1,0:T(8,128)(2,1)S(1)}, bf16[4,64,512]{2,1,0:T(8,128)(2,1)S(1)}, u32[]{:S(2)}, u32[]{:S(2)}) collective-permute-start(bf16[4,64,512]{2,1,0:T(8,128)(2,1)S(1)} %get-tuple-element.96), channel_id=1, source_target_pairs={{0,12},{1,5},{4,0},{5,9},{8,4},{9,13},{12,8},{13,1},{2,14},{3,7},{... | collective-permute-start | bytes 786440 | tf_op jit(solution)/shard_map/ppermute | solution.py:29
  69.1 12.1 %collective-permute-start.9 = (bf16[4,64,512]{2,1,0:T(8,128)(2,1)S(1)}, bf16[4,64,512]{2,1,0:T(8,128)(2,1)S(1)}, u32[]{:S(2)}, u32[]{:S(2)}) collective-permute-start(bf16[4,64,512]{2,1,0:T(8,128)(2,1)S(1)} %get-tuple-element.96), channel_id=1, source_target_pairs={{0,4},{1,13},{4,8},{5,1},{8,12},{9,5},{12,0},{13,9},{2,6},{3,15},{... | collective-permute-start | bytes 786440 | tf_op jit(solution)/shard_map/ppermute | solution.py:29
  82.2 20.1 %collective-permute-start.13 = (bf16[4,4,64,512]{3,2,1,0:T(8,128)(2,1)}, bf16[4,4,64,512]{3,2,1,0:T(8,128)(2,1)}, u32[]{:S(2)}, u32[]{:S(2)}) collective-permute-start(bf16[4,4,64,512]{3,2,1,0:T(8,128)(2,1)} %collective-permute-done.7.refs_1_), channel_id=1, source_target_pairs={{0,64},{1,193},{64,128},{65,1},{128,192},{129,65},{192,0},{193,129... | collective-permute-start | bytes 3145736 | tf_op jit(solution)/shard_map/ppermute | solution.py:29
  82.6 13.1 %collective-permute-start.12 = (bf16[4,64,512]{2,1,0:T(8,128)(2,1)S(1)}, bf16[4,64,512]{2,1,0:T(8,128)(2,1)}, u32[]{:S(2)}, u32[]{:S(2)}) collective-permute-start(bf16[4,64,512]{2,1,0:T(8,128)(2,1)S(1)} %collective-permute-done.9), channel_id=1, source_target_pairs={{0,4},{1,13},{4,8},{5,1},{8,12},{9,5},{12,0},{13,9},{2,6},{3,15},{... | collective-permute-start | bytes 786440 | tf_op jit(solution)/shard_map/ppermute | solution.py:29
  102.3 18.7 %collective-permute-start.14 = (bf16[4,4,64,512]{3,2,1,0:T(8,128)(2,1)S(1)}, bf16[4,4,64,512]{3,2,1,0:T(8,128)(2,1)}, u32[]{:S(2)}, u32[]{:S(2)}) collective-permute-start(bf16[4,4,64,512]{3,2,1,0:T(8,128)(2,1)S(1)} %pad_maximum_fusion.1.refs_0_), channel_id=1, source_target_pairs={{0,64},{1,193},{64,128},{65,1},{128,192},{129,65},{192,0},{193,129... | collective-permute-start | bytes 3145736 | tf_op jit(solution)/shard_map/ppermute | solution.py:29
  102.3 20.3 %collective-permute-start.15 = (bf16[4,4,64,512]{3,2,1,0:T(8,128)(2,1)S(1)}, bf16[4,4,64,512]{3,2,1,0:T(8,128)(2,1)}, u32[]{:S(2)}, u32[]{:S(2)}) collective-permute-start(bf16[4,4,64,512]{3,2,1,0:T(8,128)(2,1)S(1)} %pad_maximum_fusion.1.refs_0_), channel_id=1, source_target_pairs={{0,192},{1,65},{64,0},{65,129},{128,64},{129,193},{192,128},{193,1... | collective-permute-start | bytes 3145736 | tf_op jit(solution)/shard_map/ppermute | solution.py:29
  122.7 20.8 %collective-permute-start.16 = (bf16[4,4,64,512]{3,2,1,0:T(8,128)(2,1)}, bf16[4,4,64,512]{3,2,1,0:T(8,128)(2,1)S(1)}, u32[]{:S(2)}, u32[]{:S(2)}) collective-permute-start(bf16[4,4,64,512]{3,2,1,0:T(8,128)(2,1)} %collective-permute-done.14.refs_1_), channel_id=1, source_target_pairs={{0,64},{1,193},{64,128},{65,1},{128,192},{129,65},{192,0},{193,129... | collective-permute-start | bytes 3145736 | tf_op jit(solution)/shard_map/ppermute | solution.py:29
  123.9 34.0 %collective-permute-start.17 = (f32[256,512]{1,0:T(8,128)S(1)}, f32[256,512]{1,0:T(8,128)S(1)}, u32[]{:S(2)}, u32[]{:S(2)}) collective-permute-start(f32[256,512]{1,0:T(8,128)S(1)} %get-tuple-element.124), channel_id=1, source_target_pairs={{0,16},{1,49},{16,32},{17,1},{32,48},{33,17},{48,0},{49,33},{2,18}... | collective-permute-start | bytes 1572872 | tf_op jit(solution)/shard_map/ppermute | solution.py:29
  123.9 34.0 %collective-permute-start.18 = (f32[256,512]{1,0:T(8,128)S(1)}, f32[256,512]{1,0:T(8,128)S(1)}, u32[]{:S(2)}, u32[]{:S(2)}) collective-permute-start(f32[256,512]{1,0:T(8,128)S(1)} %get-tuple-element.125), channel_id=1, source_target_pairs={{0,48},{1,17},{16,0},{17,33},{32,16},{33,49},{48,32},{49,1},{2,50}... | collective-permute-start | bytes 1572872 | tf_op jit(solution)/shard_map/ppermute | solution.py:29
  127.2 30.8 %collective-permute-start.19 = (f32[256,512]{1,0:T(8,128)S(1)}, f32[256,512]{1,0:T(8,128)S(1)}, u32[]{:S(2)}, u32[]{:S(2)}) collective-permute-start(f32[256,512]{1,0:T(8,128)S(1)} %get-tuple-element.126), channel_id=1, source_target_pairs={{0,32},{1,33},{16,48},{17,49},{32,0},{33,1},{48,16},{49,17},{2,34}... | collective-permute-start | bytes 1572872 | tf_op jit(solution)/shard_map/ppermute | solution.py:29
  127.2 25.4 %collective-permute-start.20 = (bf16[2,32,3712]{2,1,0:T(8,128)(2,1)S(1)}, bf16[2,32,3712]{2,1,0:T(8,128)(2,1)S(1)}, u32[]{:S(2)}, u32[]{:S(2)}) collective-permute-start(bf16[2,32,3712]{2,1,0:T(8,128)(2,1)S(1)} %pad_maximum_fusion.3), channel_id=1, source_target_pairs={{0,4},{4,8},{8,12},{12,16},{16,20},{20,24},{24,28},{28,32},{32,36}... | collective-permute-start | bytes 1425416 | tf_op jit(solution)/shard_map/ppermute | solution.py:46
  158.0 20.0 %collective-permute-start.21 = (f32[256,512]{1,0:T(8,128)}, f32[256,512]{1,0:T(8,128)S(1)}, u32[]{:S(2)}, u32[]{:S(2)}) collective-permute-start(f32[256,512]{1,0:T(8,128)} %get-tuple-element.133), channel_id=1, source_target_pairs={{0,16},{1,49},{16,32},{17,1},{32,48},{33,17},{48,0},{49,33},{2,18}... | collective-permute-start | bytes 1572872 | tf_op jit(solution)/shard_map/ppermute | solution.py:29
  158.1 19.9 %collective-permute-start.22 = (f32[256,512]{1,0:T(8,128)}, f32[256,512]{1,0:T(8,128)}, u32[]{:S(2)}, u32[]{:S(2)}) collective-permute-start(f32[256,512]{1,0:T(8,128)} %get-tuple-element.134), channel_id=1, source_target_pairs={{0,48},{1,17},{16,0},{17,33},{32,16},{33,49},{48,32},{49,1},{2,50}... | collective-permute-start | bytes 1572872 | tf_op jit(solution)/shard_map/ppermute | solution.py:29
  161.3 16.7 %collective-permute-start.23 = (f32[256,512]{1,0:T(8,128)}, f32[256,512]{1,0:T(8,128)}, u32[]{:S(2)}, u32[]{:S(2)}) collective-permute-start(f32[256,512]{1,0:T(8,128)} %get-tuple-element.144), channel_id=1, source_target_pairs={{0,32},{1,33},{16,48},{17,49},{32,0},{33,1},{48,16},{49,17},{2,34}... | collective-permute-start | bytes 1572872 | tf_op jit(solution)/shard_map/ppermute | solution.py:29
  198.9 13.7 %collective-permute-start.24 = (f32[1,128]{1,0:T(1,128)}, f32[1,128]{1,0:T(1,128)S(1)}, u32[]{:S(2)}, u32[]{:S(2)}) collective-permute-start(f32[1,128]{1,0:T(1,128)} %get-tuple-element.148), channel_id=1, source_target_pairs={{0,4},{4,0},{8,12},{12,8},{1,5},{5,1},{9,13},{13,9},{2,6},{6,2},{1... | collective-permute-start | bytes 1544 | tf_op jit(solution)/shard_map/ppermute | solution.py:34
  198.9 13.7 %collective-permute-start.25 = (f32[1,128]{1,0:T(1,128)}, f32[1,128]{1,0:T(1,128)S(1)}, u32[]{:S(2)}, u32[]{:S(2)}) collective-permute-start(f32[1,128]{1,0:T(1,128)} %get-tuple-element.148), channel_id=1, source_target_pairs={{0,8},{4,12},{8,0},{12,4},{1,9},{5,13},{9,1},{13,5},{2,10},{6,14},... | collective-permute-start | bytes 1544 | tf_op jit(solution)/shard_map/ppermute | solution.py:34
  198.9 13.7 %collective-permute-start.26 = (f32[1,128]{1,0:T(1,128)}, f32[1,128]{1,0:T(1,128)S(1)}, u32[]{:S(2)}, u32[]{:S(2)}) collective-permute-start(f32[1,128]{1,0:T(1,128)} %get-tuple-element.148), channel_id=1, source_target_pairs={{0,12},{4,8},{8,4},{12,0},{1,13},{5,9},{9,5},{13,1},{2,14},{6,10},... | collective-permute-start | bytes 1544 | tf_op jit(solution)/shard_map/ppermute | solution.py:34
  212.7 8.1 %collective-permute-start.27 = (f32[1,128]{1,0:T(1,128)S(1)}, f32[1,128]{1,0:T(1,128)S(1)}, u32[]{:S(2)}, u32[]{:S(2)}) collective-permute-start(f32[1,128]{1,0:T(1,128)S(1)} %add_add_fusion.1), channel_id=1, source_target_pairs={{0,64},{64,0},{128,192},{192,128},{1,65},{65,1},{129,193},{193,129... | collective-permute-start | bytes 1544 | tf_op jit(solution)/shard_map/ppermute | solution.py:34
  218.0 5.0 %collective-permute-start.28 = (f32[1,128]{1,0:T(1,128)S(1)}, f32[1,128]{1,0:T(1,128)S(1)}, u32[]{:S(2)}, u32[]{:S(2)}) collective-permute-start(f32[1,128]{1,0:T(1,128)S(1)} %add_add_fusion.1), channel_id=1, source_target_pairs={{0,128},{64,192},{128,0},{192,64},{1,129},{65,193},{129,1},{193,65... | collective-permute-start | bytes 1544 | tf_op jit(solution)/shard_map/ppermute | solution.py:34
  218.0 5.0 %collective-permute-start.29 = (f32[1,128]{1,0:T(1,128)S(1)}, f32[1,128]{1,0:T(1,128)S(1)}, u32[]{:S(2)}, u32[]{:S(2)}) collective-permute-start(f32[1,128]{1,0:T(1,128)S(1)} %add_add_fusion.1), channel_id=1, source_target_pairs={{0,192},{64,128},{128,64},{192,0},{1,193},{65,129},{129,65},{193,1... | collective-permute-start | bytes 1544 | tf_op jit(solution)/shard_map/ppermute | solution.py:34
  223.2 5.1 %collective-permute-start.31 = (f32[1,128]{1,0:T(1,128)S(1)}, f32[1,128]{1,0:T(1,128)S(1)}, u32[]{:S(2)}, u32[]{:S(2)}) collective-permute-start(f32[1,128]{1,0:T(1,128)S(1)} %add_add_fusion), channel_id=1, source_target_pairs={{0,32},{16,48},{32,0},{48,16},{1,33},{17,49},{33,1},{49,17},{2,34}... | collective-permute-start | bytes 1544 | tf_op jit(solution)/shard_map/ppermute | solution.py:34
  (22 other events, 375.5 us)
Sparse Core Ops, SparseCore 0:
  40.2 57.8 all-gather.2
